TPU v7x, 32 devices: a whole 2x2x4 slice. The times are simulated.
32 devices in a mesh: batch: 8 (over z, y), mp: 4 (over x, core).
Axes of the slice: x: 2, y: 2, z: 4, core: 2. Of those that a mesh axis runs over, the one named last changes fastest.
Arguments:
- tokens: bfloat16 [784, 16, 768], P('mp', 'batch'), may hold values from -6 to 6
- segment_ids: int32 [16, 784], P('batch'), may hold values from 0 to 3, never falling along the last dimension, each value on 1 to 392 neighbouring positions
- bucket_ids: int32 [1567], replicated, may hold values from 0 to 255
- memory: bfloat16 [256, 16, 768], P('batch'), may hold values from -80 to 80
- memory_mask: int32 [16, 256], P('batch'), may hold values from 0 to 1, as said below
- cotangent: bfloat16 [784, 16, 768], P('mp', 'batch'), may hold values from -6 to 6
- self_gain: float32 [768], replicated, may hold values from 0.1 to 1.9
- self_bias: float32 [768], replicated, may hold values from -1.5 to 1.5
- query_weight: bfloat16 [768, 768], P(None, 'mp'), may hold values from -0.21875 to 0.21875
- key_weight: bfloat16 [768, 768], P(None, 'mp'), may hold values from -0.21875 to 0.21875
- value_weight: bfloat16 [768, 768], P(None, 'mp'), may hold values from -0.21875 to 0.21875
- rel_table: float32 [256, 12], P(None, 'mp'), may hold values from -4 to 4
- head_scale: float32 [12], P('mp'), may hold values from 0.1 to 1.9
- output_weight: bfloat16 [768, 768], P('mp'), may hold values from -0.21875 to 0.21875
- after_gain: float32 [768], replicated, may hold values from 0.1 to 1.9
- after_bias: float32 [768], replicated, may hold values from -1.5 to 1.5
- cross_gain: float32 [768], replicated, may hold values from 0.1 to 1.9
- cross_bias: float32 [768], replicated, may hold values from -1.5 to 1.5
- batch_gain: float32 [768], replicated, may hold values from 0.1 to 1.9
- batch_bias: float32 [768], replicated, may hold values from -1.5 to 1.5
- cross_query: bfloat16 [768, 768], P(None, 'mp'), may hold values from -0.21875 to 0.21875
- cross_key: bfloat16 [768, 768], P(None, 'mp'), may hold values from -0.21875 to 0.21875
- cross_value: bfloat16 [768, 768], P(None, 'mp'), may hold values from -0.21875 to 0.21875
- cross_output: bfloat16 [768, 768], P('mp'), may hold values from -0.21875 to 0.21875
- crossout_gain: float32 [768], replicated, may hold values from 0.1 to 1.9
- crossout_bias: float32 [768], replicated, may hold values from -1.5 to 1.5
- ffn_gain: float32 [768], replicated, may hold values from 0.1 to 1.9
- ffn_bias: float32 [768], replicated, may hold values from -1.5 to 1.5
- up_weight: bfloat16 [768, 3072], P(None, 'mp'), may hold values from -2 to 2
- middle_gain: float32 [3072], P('mp'), may hold values from 0.1 to 1.9
- middle_bias: float32 [3072], P('mp'), may hold values from -1.5 to 1.5
- down_weight: bfloat16 [3072, 768], P('mp'), may hold values from -0.109375 to 0.109375
Outputs:
- output: bfloat16 [784, 16, 768], P('mp', 'batch')
- grad_tokens: float32 [784, 16, 768], P('mp', 'batch')
- grad_memory: float32 [256, 16, 768], P('batch', None, 'mp')
- grad_self_gain: float32 [768], replicated
- grad_self_bias: float32 [768], replicated
- grad_query_weight: float32 [768, 768], P(None, 'mp')
- grad_key_weight: float32 [768, 768], P(None, 'mp')
- grad_value_weight: float32 [768, 768], P(None, 'mp')
- grad_rel_table: float32 [256, 12], P(None, 'mp')
- grad_head_scale: float32 [12], P('mp')
- grad_output_weight: float32 [768, 768], P('mp')
- grad_after_gain: float32 [768], replicated
- grad_after_bias: float32 [768], replicated
- grad_cross_gain: float32 [768], replicated
- grad_cross_bias: float32 [768], replicated
- grad_batch_gain: float32 [768], P('mp')
- grad_batch_bias: float32 [768], P('mp')
- grad_cross_query: float32 [768, 768], P(None, 'mp')
- grad_cross_key: float32 [768, 768], P(None, 'mp')
- grad_cross_value: float32 [768, 768], P(None, 'mp')
- grad_cross_output: float32 [768, 768], P('mp')
- grad_crossout_gain: float32 [768], replicated
- grad_crossout_bias: float32 [768], replicated
- grad_ffn_gain: float32 [768], replicated
- grad_ffn_bias: float32 [768], replicated
- grad_up_weight: float32 [768, 3072], P(None, 'mp')
- grad_middle_gain: float32 [3072], P('mp')
- grad_middle_bias: float32 [3072], P('mp')
- grad_down_weight: float32 [3072, 768], P('mp')
Inputs may be any that keep to these rules, and one draw needn't show every extreme that they name: `segment_ids`: ids of a row never fall. `memory_mask`: the valid positions of each sample form a prefix of at least 64 positions.
All inputs are finite; a program needn't handle non-finite values.
Results may differ from a plain program's by a relative error of at most 0.02.
The roundings to bfloat16 on the way count: a program that leaves them out, or rounds other values in their place, can miss the bound.
Values may be sent and summed in bfloat16 or wider, within the bound.
No kernel may reach another device: no remote copies, remote signals or barrier semaphores. Data moves between devices by JAX's collectives and lax.ppermute only.
A program may use at most 256 MiB of HBM per device.

v0:
```python
import jax
import jax.numpy as jnp
from jax import lax
from jax.sharding import PartitionSpec as P

HEAD_DIM = 64
FF = 3072
MEM = 256


EPSILON = 1e-05
MASKED = -1e30


def layer_norm(values, gain, bias):
    center = values - jnp.mean(values, -1, keepdims=True)
    spread = jnp.mean(center * center, -1, keepdims=True)
    return center * lax.rsqrt(spread + EPSILON) * gain + bias


def norm_back(values, gain, bias, upstream):
    return jax.vjp(layer_norm, values, gain, bias)[1](upstream)


def gelu_exact(values):
    return jax.nn.gelu(values, approximate=False)


def project(left, weight):
    return jnp.einsum("srd,dc->src", left, weight, preferred_element_type=jnp.float32)


def spread_rows(shard):
    return lax.all_gather(shard, "mp", axis=0, tiled=True)


def combine_rows(pairs, form):
    total = None
    for left, weight in pairs:
        piece = jnp.einsum(form, left, weight, preferred_element_type=jnp.float32)
        total = piece if total is None else total + piece
    return lax.psum_scatter(total, "mp", scatter_dimension=0, tiled=True)


def middle_sums(first, second):
    return lax.psum((jnp.sum(first, -1), jnp.sum(second, -1)), "mp")


def bucket_choice(table, bucket_ids):
    return (bucket_ids[:, None] == jnp.arange(table.shape[0])[None, :]).astype(jnp.float32)


def position_bias(choose, table, length):
    by_offset = jnp.dot(choose, table, precision=lax.Precision.HIGHEST)
    count_heads = table.shape[1]
    reversed_rows = jnp.flip(by_offset, 0).T
    repeated = jnp.broadcast_to(
        reversed_rows[:, None, :], (count_heads, length, 2 * length - 1)
    ).reshape(count_heads, length * (2 * length - 1))
    padded = jnp.pad(repeated, ((0, 0), (0, length)))
    skewed = padded.reshape(count_heads, length, 2 * length)[:, :, :length]
    return jnp.flip(skewed, -1)


def offset_sums(choose, grad_bias, length):
    count_heads = grad_bias.shape[0]
    flipped = jnp.flip(grad_bias, -1)
    padded = jnp.pad(flipped, ((0, 0), (0, 0), (0, length)))
    flattened = padded.reshape(count_heads, 2 * length * length)[:, : length * (2 * length - 1)]
    skewed = flattened.reshape(count_heads, length, 2 * length - 1)
    column_sums = jnp.sum(skewed, 1)
    by_offset = jnp.flip(column_sums, -1).T
    return jnp.dot(choose.T, by_offset, precision=lax.Precision.HIGHEST)


def self_mask(segment):
    places = jnp.arange(segment.shape[0])
    return (places[None, :] <= places[:, None]) & (segment[None, :] == segment[:, None])


def head_split(block, heads):
    return block.reshape(block.shape[0], heads, block.shape[1] // heads)


def pick_row(block, row):
    return lax.dynamic_index_in_dim(block, row, 1, keepdims=False)


def attend_forward(query, key, value, bias, allowed, heads):
    scale = HEAD_DIM ** (-0.5)
    products = jnp.einsum(
        "ihe,jhe->hij",
        head_split(query, heads),
        head_split(key, heads),
        preferred_element_type=jnp.float32,
    )
    scores = jnp.where(allowed, products * scale + bias, MASKED)
    peak = jnp.max(scores, -1, keepdims=True)
    shifted = jnp.exp(scores - peak)
    total = jnp.sum(shifted, -1, keepdims=True)
    weights = (shifted / total).astype(jnp.bfloat16)
    mixed = jnp.einsum(
        "hij,jhe->ihe", weights, head_split(value, heads), preferred_element_type=jnp.float32
    )
    return (mixed.reshape(mixed.shape[0], -1), peak, total)


def attend_backward(query, key, value, bias, allowed, peak, total, upstream, heads):
    scale = HEAD_DIM ** (-0.5)
    query_heads = head_split(query, heads)
    key_heads = head_split(key, heads)
    value_heads = head_split(value, heads)
    grad_heads = head_split(upstream, heads)
    products = jnp.einsum(
        "ihe,jhe->hij", query_heads, key_heads, preferred_element_type=jnp.float32
    )
    scores = jnp.where(allowed, products * scale + bias, MASKED)
    probs = jnp.exp(scores - peak) / total
    weights = probs.astype(jnp.bfloat16)
    grad_probs = jnp.einsum(
        "ihe,jhe->hij", grad_heads, value_heads, preferred_element_type=jnp.float32
    )
    inner = jnp.sum(probs * grad_probs, -1, keepdims=True)
    grad_scores = (probs * (grad_probs - inner)).astype(jnp.bfloat16)
    grad_query = (
        jnp.einsum("hij,jhe->ihe", grad_scores, key_heads, preferred_element_type=jnp.float32)
        * scale
    ).astype(jnp.bfloat16)
    grad_key = (
        jnp.einsum("hij,ihe->jhe", grad_scores, query_heads, preferred_element_type=jnp.float32)
        * scale
    ).astype(jnp.bfloat16)
    grad_value = jnp.einsum(
        "hij,ihe->jhe", weights, grad_heads, preferred_element_type=jnp.float32
    ).astype(jnp.bfloat16)
    return (
        grad_query.reshape(grad_query.shape[0], -1),
        grad_key.reshape(grad_key.shape[0], -1),
        grad_value.reshape(grad_value.shape[0], -1),
        grad_scores,
    )


def on_device(
    tokens,
    segment_ids,
    bucket_ids,
    memory,
    memory_mask,
    cotangent,
    self_gain,
    self_bias,
    query_weight,
    key_weight,
    value_weight,
    rel_table,
    head_scale,
    output_weight,
    after_gain,
    after_bias,
    cross_gain,
    cross_bias,
    batch_gain,
    batch_bias,
    cross_query,
    cross_key,
    cross_value,
    cross_output,
    crossout_gain,
    crossout_bias,
    ffn_gain,
    ffn_bias,
    up_weight,
    middle_gain,
    middle_bias,
    down_weight,
):
    heads = rel_table.shape[1]
    rows = tokens.shape[1]
    length = tokens.shape[0] * lax.axis_size("mp")
    stream = tokens.astype(jnp.float32)
    self_in = spread_rows(layer_norm(stream, self_gain, self_bias).astype(jnp.bfloat16))
    queries = project(self_in, query_weight).astype(jnp.bfloat16)
    keys = project(self_in, key_weight).astype(jnp.bfloat16)
    values = project(self_in, value_weight).astype(jnp.bfloat16)
    choose = bucket_choice(rel_table, bucket_ids)
    table_bias = position_bias(choose, rel_table, length)

    def self_step(row):
        segment = lax.dynamic_index_in_dim(segment_ids, row, 0, keepdims=False)
        return attend_forward(
            pick_row(queries, row),
            pick_row(keys, row),
            pick_row(values, row),
            table_bias,
            self_mask(segment)[None],
            heads,
        )

    mixed_rows, peaks, totals = lax.map(self_step, jnp.arange(rows))
    mixed = jnp.moveaxis(mixed_rows, 0, 1)
    scale_lanes = jnp.repeat(head_scale, HEAD_DIM)
    scaled = (mixed * scale_lanes).astype(jnp.bfloat16)
    attn_sum = combine_rows(((scaled, output_weight),), "src,cd->srd")
    first = stream + layer_norm(attn_sum, after_gain, after_bias)
    cross_in = spread_rows(layer_norm(first, cross_gain, cross_bias).astype(jnp.bfloat16))
    cross_queries = project(cross_in, cross_query).astype(jnp.bfloat16)
    mem_float = memory.astype(jnp.float32)
    count = MEM * memory.shape[1]
    mem_sum, mem_square = lax.psum(
        (jnp.sum(mem_float, (0, 1)), jnp.sum(mem_float * mem_float, (0, 1))), "batch"
    )
    mem_mean = mem_sum / count
    mem_scale = lax.rsqrt(mem_square / count - mem_mean * mem_mean + EPSILON)
    mem_hat = (mem_float - mem_mean) * mem_scale
    normed = (mem_hat * batch_gain + batch_bias).astype(jnp.bfloat16)
    mem_keys, mem_values = (
        lax.all_to_all(
            project(normed, cross_key).astype(jnp.bfloat16),
            "batch",
            split_axis=1,
            concat_axis=0,
            tiled=True,
        ),
        lax.all_to_all(
            project(normed, cross_value).astype(jnp.bfloat16),
            "batch",
            split_axis=1,
            concat_axis=0,
            tiled=True,
        ),
    )

    def cross_step(row):
        valid = lax.dynamic_index_in_dim(memory_mask, row, 0, keepdims=False)
        return attend_forward(
            pick_row(cross_queries, row),
            pick_row(mem_keys, row),
            pick_row(mem_values, row),
            0.0,
            (valid > 0)[None, None, :],
            heads,
        )

    cross_rows, cross_peaks, cross_totals = lax.map(cross_step, jnp.arange(rows))
    cross_mixed = jnp.moveaxis(cross_rows, 0, 1).astype(jnp.bfloat16)
    cross_sum = combine_rows(((cross_mixed, cross_output),), "src,cd->srd")
    second = first + layer_norm(cross_sum, crossout_gain, crossout_bias)
    ffn_in = spread_rows(layer_norm(second, ffn_gain, ffn_bias).astype(jnp.bfloat16))
    gate = project(ffn_in, up_weight)
    active = gelu_exact(gate)
    act_sum, act_square = middle_sums(active, active * active)
    act_mean = act_sum / FF
    act_scale = lax.rsqrt(act_square / FF - act_mean * act_mean + EPSILON)
    act_hat = (active - act_mean[..., None]) * act_scale[..., None]
    middle = (act_hat * middle_gain + middle_bias).astype(jnp.bfloat16)
    ffn_sum = combine_rows(((middle, down_weight),), "src,cd->srd")
    output = (second + ffn_sum).astype(jnp.bfloat16)
    upstream = cotangent.astype(jnp.float32)
    grad_all = spread_rows(cotangent)
    grad_down = jnp.einsum("src,srd->cd", middle, grad_all, preferred_element_type=jnp.float32)
    grad_middle = jnp.einsum(
        "srd,cd->src", grad_all, down_weight, preferred_element_type=jnp.float32
    )
    grad_mid_gain = jnp.sum(grad_middle * act_hat, (0, 1))
    grad_mid_bias = jnp.sum(grad_middle, (0, 1))
    grad_hat = grad_middle * middle_gain
    hat_sum, hat_cross = middle_sums(grad_hat, grad_hat * act_hat)
    grad_active = act_scale[..., None] * (
        grad_hat - hat_sum[..., None] / FF - act_hat * hat_cross[..., None] / FF
    )
    grad_gate = jax.vjp(gelu_exact, gate)[1](grad_active)[0].astype(jnp.bfloat16)
    grad_up = jnp.einsum("srd,src->dc", ffn_in, grad_gate, preferred_element_type=jnp.float32)
    grad_ffn_in = combine_rows(((grad_gate, up_weight),), "src,dc->srd")
    back_second, grad_ffn_gain, grad_ffn_bias = norm_back(second, ffn_gain, ffn_bias, grad_ffn_in)
    grad_second = upstream + back_second
    grad_cross_sum, grad_co_gain, grad_co_bias = norm_back(
        cross_sum, crossout_gain, crossout_bias, grad_second
    )
    grad_cross_all = spread_rows(grad_cross_sum.astype(jnp.bfloat16))
    grad_coutput = jnp.einsum(
        "src,srd->cd", cross_mixed, grad_cross_all, preferred_element_type=jnp.float32
    )
    grad_cross_mixed = jnp.einsum(
        "srd,cd->src", grad_cross_all, cross_output, preferred_element_type=jnp.float32
    ).astype(jnp.bfloat16)

    def cross_back(row):
        valid = lax.dynamic_index_in_dim(memory_mask, row, 0, keepdims=False)
        outcome = attend_backward(
            pick_row(cross_queries, row),
            pick_row(mem_keys, row),
            pick_row(mem_values, row),
            0.0,
            (valid > 0)[None, None, :],
            cross_peaks[row],
            cross_totals[row],
            pick_row(grad_cross_mixed, row),
            heads,
        )
        return (outcome[0], outcome[1], outcome[2])

    grad_cq_rows, grad_mk_rows, grad_mv_rows = lax.map(cross_back, jnp.arange(rows))
    grad_cq = jnp.moveaxis(grad_cq_rows, 0, 1)
    grad_mem_keys = jnp.moveaxis(grad_mk_rows, 0, 1)
    grad_mem_values = jnp.moveaxis(grad_mv_rows, 0, 1)
    grad_cquery = jnp.einsum("srd,src->dc", cross_in, grad_cq, preferred_element_type=jnp.float32)
    grad_cross_in = combine_rows(((grad_cq, cross_query),), "src,dc->srd")
    back_first, grad_cross_gain, grad_cross_bias = norm_back(
        first, cross_gain, cross_bias, grad_cross_in
    )
    grad_first = grad_second + back_first
    back_keys, back_values = (
        lax.all_to_all(grad_mem_keys, "batch", split_axis=0, concat_axis=1, tiled=True),
        lax.all_to_all(grad_mem_values, "batch", split_axis=0, concat_axis=1, tiled=True),
    )
    grad_ckey = jnp.einsum("mrd,mrc->dc", normed, back_keys, preferred_element_type=jnp.float32)
    grad_cvalue = jnp.einsum("mrd,mrc->dc", normed, back_values, preferred_element_type=jnp.float32)
    grad_normed = jnp.einsum(
        "mrc,dc->mrd", back_keys, cross_key, preferred_element_type=jnp.float32
    ) + jnp.einsum("mrc,dc->mrd", back_values, cross_value, preferred_element_type=jnp.float32)
    grad_mem_part = lax.psum_scatter(grad_normed, "mp", scatter_dimension=2, tiled=True)
    channels = grad_mem_part.shape[2]
    offset = lax.axis_index("mp") * channels
    hat_slice = lax.dynamic_slice_in_dim(mem_hat, offset, channels, 2)
    gain_slice = lax.dynamic_slice_in_dim(batch_gain, offset, channels, 0)
    scale_slice = lax.dynamic_slice_in_dim(mem_scale, offset, channels, 0)
    shift_term = jnp.sum(grad_mem_part, (0, 1))
    scale_term = jnp.sum(grad_mem_part * hat_slice, (0, 1))
    grad_attn_sum, grad_after_gain, grad_after_bias = norm_back(
        attn_sum, after_gain, after_bias, grad_first
    )
    grad_attn_all = spread_rows(grad_attn_sum.astype(jnp.bfloat16))
    grad_output = jnp.einsum(
        "src,srd->cd", scaled, grad_attn_all, preferred_element_type=jnp.float32
    )
    grad_scaled = jnp.einsum(
        "srd,cd->src", grad_attn_all, output_weight, preferred_element_type=jnp.float32
    )
    grad_scale = jnp.sum((grad_scaled * mixed).reshape(length, rows, heads, HEAD_DIM), (0, 1, 3))
    grad_mixed = (grad_scaled * scale_lanes).astype(jnp.bfloat16)

    def self_back(bias_grad, row):
        segment = lax.dynamic_index_in_dim(segment_ids, row, 0, keepdims=False)
        outcome = attend_backward(
            pick_row(queries, row),
            pick_row(keys, row),
            pick_row(values, row),
            table_bias,
            self_mask(segment)[None],
            peaks[row],
            totals[row],
            pick_row(grad_mixed, row),
            heads,
        )
        return (bias_grad + outcome[3].astype(jnp.float32), (outcome[0], outcome[1], outcome[2]))

    bias_grad, (grad_q_rows, grad_k_rows, grad_v_rows) = lax.scan(
        self_back, jnp.zeros((heads, length, length), jnp.float32), jnp.arange(rows)
    )
    grad_table = offset_sums(choose, bias_grad, length)
    grad_queries = jnp.moveaxis(grad_q_rows, 0, 1)
    grad_keys = jnp.moveaxis(grad_k_rows, 0, 1)
    grad_values = jnp.moveaxis(grad_v_rows, 0, 1)
    grad_query = jnp.einsum(
        "srd,src->dc", self_in, grad_queries, preferred_element_type=jnp.float32
    )
    grad_key = jnp.einsum("srd,src->dc", self_in, grad_keys, preferred_element_type=jnp.float32)
    grad_value = jnp.einsum("srd,src->dc", self_in, grad_values, preferred_element_type=jnp.float32)
    grad_self_in = combine_rows(
        ((grad_queries, query_weight), (grad_keys, key_weight), (grad_values, value_weight)),
        "src,dc->srd",
    )
    back_tokens, grad_self_gain, grad_self_bias = norm_back(
        stream, self_gain, self_bias, grad_self_in
    )
    grad_tokens = grad_first + back_tokens
    (
        sum_query,
        sum_key,
        sum_value,
        sum_table,
        sum_scale,
        sum_output,
        sum_cquery,
        sum_ckey,
        sum_cvalue,
        sum_coutput,
        sum_up,
        sum_down,
        sum_mid_gain,
        sum_mid_bias,
        shift_total,
        scale_total,
    ) = lax.psum(
        (
            grad_query,
            grad_key,
            grad_value,
            grad_table,
            grad_scale,
            grad_output,
            grad_cquery,
            grad_ckey,
            grad_cvalue,
            grad_coutput,
            grad_up,
            grad_down,
            grad_mid_gain,
            grad_mid_bias,
            shift_term,
            scale_term,
        ),
        "batch",
    )
    grad_memory = (
        gain_slice
        * scale_slice
        * (grad_mem_part - shift_total / count - hat_slice * scale_total / count)
    )
    norm_totals = lax.psum(
        (
            grad_self_gain,
            grad_self_bias,
            grad_after_gain,
            grad_after_bias,
            grad_cross_gain,
            grad_cross_bias,
            grad_co_gain,
            grad_co_bias,
            grad_ffn_gain,
            grad_ffn_bias,
        ),
        ("batch", "mp"),
    )
    return (
        output,
        grad_tokens,
        grad_memory,
        norm_totals[0],
        norm_totals[1],
        sum_query,
        sum_key,
        sum_value,
        sum_table,
        sum_scale,
        sum_output,
        norm_totals[2],
        norm_totals[3],
        norm_totals[4],
        norm_totals[5],
        scale_total,
        shift_total,
        sum_cquery,
        sum_ckey,
        sum_cvalue,
        sum_coutput,
        norm_totals[6],
        norm_totals[7],
        norm_totals[8],
        norm_totals[9],
        sum_up,
        sum_mid_gain,
        sum_mid_bias,
        sum_down,
    )


def solution(mesh):
    in_specs = (
        P("mp", "batch", None),
        P("batch", None),
        P(),
        P("batch", None, None),
        P("batch", None),
        P("mp", "batch", None),
        P(),
        P(),
        P(None, "mp"),
        P(None, "mp"),
        P(None, "mp"),
        P(None, "mp"),
        P("mp"),
        P("mp", None),
        P(),
        P(),
        P(),
        P(),
        P(),
        P(),
        P(None, "mp"),
        P(None, "mp"),
        P(None, "mp"),
        P("mp", None),
        P(),
        P(),
        P(),
        P(),
        P(None, "mp"),
        P("mp"),
        P("mp"),
        P("mp", None),
    )
    out_specs = (
        P("mp", "batch", None),
        P("mp", "batch", None),
        P("batch", None, "mp"),
        P(),
        P(),
        P(None, "mp"),
        P(None, "mp"),
        P(None, "mp"),
        P(None, "mp"),
        P("mp"),
        P("mp", None),
        P(),
        P(),
        P(),
        P(),
        P("mp"),
        P("mp"),
        P(None, "mp"),
        P(None, "mp"),
        P(None, "mp"),
        P("mp", None),
        P(),
        P(),
        P(),
        P(),
        P(None, "mp"),
        P("mp"),
        P("mp"),
        P("mp", None),
    )
    return jax.shard_map(
        on_device, mesh=mesh, in_specs=in_specs, out_specs=out_specs, check_vma=False
    )
```

profile of v0, /device:TPU:0, one launch (start us, length us, event | category | flops | bytes accessed | tf_op | source)
XLA Modules:
  0.0 1605.7 jit_solution(14013754478683992817)
XLA Ops:
  16.6 6.4 broadcast_in_dim.124
  23.0 25.1 %reshape.477 = f32[3685584]{0:T(1024)} reshape(f32[3,784,1567]{2,1,0:T(8,128)} %broadcast_in_dim.124) | data formatting | bytes 29484672
  48.1 22.5 %reshape.437 = f32[3,1228528]{1,0:T(4,128)} reshape(f32[3685584]{0:T(1024)} %reshape.477) | data formatting | bytes 29484672 | tf_op jit(solution)/shard_map/reshape | solution.py:59
  70.6 19.0 %pad.8 = f32[3,1229312]{1,0:T(4,128)} pad(f32[3,1228528]{1,0:T(4,128)} %reshape.437, f32[]{:T(128)} %constant.205.clone.1), padding=0_0x0_784 | pad | bytes 29494084 | tf_op jit(solution)/shard_map/jit(_pad)/pad | solution.py:60
  89.6 42.2 %reshape.479 = f32[3687936]{0:T(1024)} reshape(f32[3,1229312]{1,0:T(4,128)} %pad.8) | data formatting | bytes 29503488
  131.8 17.4 %reshape.438 = f32[3,784,1568]{2,1,0:T(8,128)} reshape(f32[3687936]{0:T(1024)} %reshape.479) | data formatting | bytes 29503488 | tf_op jit(solution)/shard_map/reshape | solution.py:61
  149.2 7.2 slice.8
  156.4 76.2 %reverse.1 = f32[3,784,896]{2,1,0:T(8,128)} reverse(f32[3,784,896]{2,1,0:T(8,128)} %bitcast.405), dimensions={2} | reverse | bytes 16859136
  232.6 8.9 slice.11
  241.5 10.4 copy.264
  257.0 24.8 %while.63 = (s32[]{:T(128)}, f32[2,784,192]{1,2,0:T(8,128)}, f32[2,3,784,1]{2,1,3,0:T(4,128)S(1)}, f32[2,3,784,1]{2,1,3,0:T(4,128)S(1)}, s32[2]{0:T(128)S(1)}, /...) while((s32[]{:T(128)}, f32[2,784,192]{1,2,0:T(8,128)}, ...), condition=%wide.region_5.6_spmd.clone, body=%wide.region_2.5_spmd.sunk.clone | while | flops 490490784 | bytes 35449124 | solution.py:200
  260.5 5.4 fusion.273
  272.8 5.4 fusion.273
  285.0 5.9 copy.265
  292.8 96.5 %all-reduce.22.cloned.1.call-done = f32[784,2,768]{2,1,0:T(2,128)} async-done(((f32[784,2,768]{2,1,0:T(2,128)}), f32[784,2,768]{2,1,0:T(2,128)}) %all-reduce.22.cloned.1.call-update) | async-done | bytes 4816912
  400.8 21.8 %all-reduce.10 = (f32[768]{0:T(1024)S(1)}, f32[768]{0:T(1024)S(1)}) all-reduce(f32[768]{0:T(1024)S(1)} %get-tuple-element.637, f32[768]{0:T(1024)S(1)} %get-tuple-element.636), channel_id=1, replica_groups=mesh['batch'=8,'mp'=4] {'batch'}, use_global_device_ids=true, to_apply=%region_14.15 | all-reduce | flops 1536 | bytes 12288 | tf_op jit(solution)/shard_map/psum | solution.py:210
  429.6 6.9 all-to-all-done
  440.2 7.9 all-to-all-done.1
  451.0 10.6 while.64
  462.6 6.0 copy.281
  468.6 93.1 %all-reduce.24.cloned.1.call-done = f32[784,2,768]{2,1,0:T(2,128)} async-done(((f32[784,2,768]{2,1,0:T(2,128)}), f32[784,2,768]{2,1,0:T(2,128)}) %all-reduce.24.cloned.1.call-update) | async-done | bytes 4816912
  578.0 24.0 %all-gather.11.cloned.1.call-done = bf16[784,2,768]{2,1,0:T(2,128)(2,1)} async-done(((bf16[196,2,768]{2,1,0:T(2,128)(2,1)}), bf16[784,2,768]{2,1,0:T(2,128)(2,1)}) %all-gather.11.cloned.1.call-update) | async-done | bytes 2408464 | tf_op jit(solution)/shard_map/all_gather | solution.py:34
  602.0 6.8 fusion.84
  608.9 14.7 fusion.141
  623.5 10.8 all-reduce.13
  635.7 9.3 multiply_reduce_fusion.2
  645.0 11.8 all-reduce.12
  657.5 8.4 add_convert_fusion
  668.0 5.9 copy.293
  674.0 97.3 %all-reduce.26.cloned.1.call-done = f32[784,2,768]{2,1,0:T(2,128)} async-done(((f32[784,2,768]{2,1,0:T(2,128)}), f32[784,2,768]{2,1,0:T(2,128)}) %all-reduce.26.cloned.1.call-update) | async-done | bytes 4816912
  779.2 5.4 multiply_reduce_fusion.7
  789.9 24.6 %all-gather.15.cloned.1.call-done = bf16[784,2,768]{2,1,0:T(2,128)(2,1)} async-done(((bf16[196,2,768]{2,1,0:T(2,128)(2,1)}), bf16[784,2,768]{2,1,0:T(2,128)(2,1)}) %all-gather.15.cloned.1.call-update) | async-done | bytes 2408464 | tf_op jit(solution)/shard_map/all_gather | solution.py:34
  818.1 17.2 %while.65 = (s32[]{:T(128)}, bf16[2,784,192]{1,2,0:T(8,128)(2,1)S(1)}, bf16[2,256,192]{1,2,0:T(8,128)(2,1)S(1)}, bf16[2,256,192]{1,2,0:T(8,128)(2,1)}, s32[2]{0:...) while((s32[]{:T(128)}, ...), condition=%wide.region_40.41_spmd.clone, body=%wide.region_38.40_spmd.sunk.clone | while | flops 391819200 | bytes 24388856 | solution.py:303
  836.3 5.9 copy.305
  842.2 95.7 %all-reduce.28.cloned.1.call-done = f32[784,2,768]{2,1,0:T(2,128)} async-done(((f32[784,2,768]{2,1,0:T(2,128)}), f32[784,2,768]{2,1,0:T(2,128)}) %all-reduce.28.cloned.1.call-update) | async-done | bytes 4816912
  937.9 4.3 multiply_reduce_fusion.8
  945.9 4.7 multiply_reduce_fusion.9
  956.7 5.5 all-to-all-start.3
  963.1 7.9 all-to-all-done.3
  974.7 5.1 fusion.87
  979.7 5.9 copy.291
  987.6 10.5 copy.340
  998.1 11.6 reshape.465
  1009.9 4.7 fusion.60
  1017.4 66.1 %while.66 = (s32[]{:T(128)}, f32[3,784,784]{1,2,0:T(8,128)}, bf16[2,784,192]{1,2,0:T(8,128)(2,1)}, bf16[2,784,192]{1,2,0:T(8,128)(2,1)}, bf16[2,784,192]{1,2,0:T...) while((s32[]{:T(128)}, f32[3,784,784]{1,2,0:T(8,128)}, ...), condition=%wide.region_48.49_spmd.clone.clone, body=%wide.region_46.48_spmd.clone.sunk.clone | while | flops 1208549376 | bytes 184346208 | solution.py:358
  1027.3 5.8 multiply_reduce_fusion.25
  1033.0 10.4 select_add_fusion.3
  1059.1 5.8 multiply_reduce_fusion.25
  1064.9 12.7 select_add_fusion.3
  1088.6 5.9 copy.316
  1094.8 6.3 fusion.49
  1101.2 7.0 fusion.52
  1133.7 72.6 %rev.17 = f32[3,784,784]{1,2,0:T(8,128)} reverse(f32[3,784,784]{1,2,0:T(8,128)} %get-tuple-element.283), dimensions={2} | reverse | bytes 14751744 | tf_op jit(solution)/shard_map/jit(_flip)/rev | solution.py:67
  1206.3 10.4 copy.343
  1216.7 10.3 pad.9.clone
  1227.0 18.4 %reshape.481 = f32[3687936]{0:T(1024)} reshape(f32[3,784,1568]{2,1,0:T(8,128)} %pad.9.clone) | data formatting | bytes 29503488
  1245.4 21.5 %reshape.439 = f32[3,1229312]{1,0:T(4,128)} reshape(f32[3687936]{0:T(1024)} %reshape.481) | data formatting | bytes 29503488 | tf_op jit(solution)/shard_map/reshape | solution.py:69
  1266.9 17.4 %slice.9 = f32[3,1228528]{1,0:T(4,128)} slice(f32[3,1229312]{1,0:T(4,128)} %reshape.439), slice={[0:3], [0:1228528]} | slice | bytes 29484672 | tf_op jit(solution)/shard_map/slice | solution.py:69
  1284.3 44.8 %reshape.483 = f32[3685584]{0:T(1024)} reshape(f32[3,1228528]{1,0:T(4,128)} %slice.9) | data formatting | bytes 29484672
  1329.1 25.6 %reshape.440 = f32[3,784,1567]{2,1,0:T(8,128)} reshape(f32[3685584]{0:T(1024)} %reshape.483) | data formatting | bytes 29484672 | tf_op jit(solution)/shard_map/reshape | solution.py:70
  1354.8 6.4 reduce_sum.472
  1363.3 40.1 %all-reduce.9 = (f32[192]{0:T(256)S(1)}, f32[192]{0:T(256)S(1)}, f32[256,3]{0,1:T(4,128)}, f32[3]{0:T(128)}, f32[768]{0:T(1024)}, /*index=5*/f32[768]{0:T(1024)}) all-reduce(f32[192]{0:T(256)S(1)} %multiply_reduce_fusion.19, f32[192]{0:T(256)S(1)} %bitcast_reduce_fusion, ...), channel_id=1, replica_groups=mesh['batch'=8,'mp'=4] {'batch'}, use_global_device_ids=true, to_apply=%region_56.57 | all-reduce | flops 2691 | bytes 21528 | tf_op jit(solution)/shard_map/psum | solution.py:395
  1408.3 40.0 %all-reduce.8 = (f32[768]{0:T(1024)}, f32[768]{0:T(1024)}, f32[768]{0:T(1024)}, f32[768]{0:T(1024)}, f32[768]{0:T(1024)}, /*index=5*/f32[768]{0:T(1024)}, f32[76...) all-reduce(f32[768]{0:T(1024)S(1)} %get-tuple-element.622, ...), channel_id=1, replica_groups=mesh['batch'=8,'mp'=4] {'batch','mp'}, use_global_device_ids=true, to_apply=%region_58.59 | all-reduce | flops 7680 | bytes 61440 | tf_op jit(solution)/shard_map/psum | solution.py:421
  1455.9 130.0 %all-reduce.30.cloned.1.call-done = (f32[768,192]{0,1:T(8,128)}, f32[768,192]{0,1:T(8,128)}, f32[768,192]{0,1:T(8,128)}, f32[192,768]{1,0:T(8,128)}, f32[768,192...) async-done(((f32[768,192]{0,1:T(8,128)}, f32[768,192]{0,1:T(8,128)}, ...) | async-done | bytes 9437200 | tf_op jit(solution)/shard_map/psum | solution.py:395
  (594 shorter events, 215.4 us)
Async XLA Ops:
  7.2 594.8 %copy-start = (bf16[768,768]{1,0:T(8,128)(2,1)S(1)}, bf16[768,768]{1,0:T(8,128)(2,1)}, u32[]{:S(2)}) copy-start(bf16[768,768]{1,0:T(8,128)(2,1)} %param.68) | copy-start | bytes 3538948
  7.2 244.8 %all-gather.7.cloned.1.call-start = ((), (), s32[]{:S(2)}) async-start(), calls=%async_computation.5 | async-start | bytes 3010560 | tf_op jit(solution)/shard_map/all_gather | solution.py:34
  9.0 14.0 copy-start.40
  14.4 374.9 %all-reduce.22.cloned.1.call-start = ((), (), s32[]{:S(2)}) async-start(), calls=%async_computation.12 | async-start | bytes 9633792
  252.1 29.8 %copy-start.125 = (f32[192]{0:T(256)}, f32[192]{0:T(256)S(1)}, u32[]{:S(2)}) copy-start(f32[192]{0:T(256)S(1)} %mul.481) | copy-start | bytes 2308
  291.0 103.0 %copy-start.9 = (bf16[196,2,768]{2,1,0:T(2,128)(2,1)S(1)}, bf16[196,2,768]{2,1,0:T(2,128)(2,1)}, u32[]{:S(2)}) copy-start(bf16[196,2,768]{2,1,0:T(2,128)(2,1)} %param.40) | copy-start | bytes 1806340
  291.0 103.0 %copy-start.92 = (f32[768]{0:T(1024)S(1)}, f32[768]{0:T(1024)}, u32[]{:S(2)}) copy-start(f32[768]{0:T(1024)} %param.54) | copy-start | bytes 9220
  291.0 103.0 %copy-start.118 = (f32[768]{0:T(1024)S(1)}, f32[768]{0:T(1024)}, u32[]{:S(2)}) copy-start(f32[768]{0:T(1024)} %param.55) | copy-start | bytes 9220
  291.0 157.3 %all-gather.9.cloned.1.call-start = ((), (), s32[]{:S(2)}) async-start(), calls=%async_computation.6 | async-start | bytes 3010560 | tf_op jit(solution)/shard_map/all_gather | solution.py:34
  397.6 25.1 %copy-start.132 = (f32[768]{0:T(1024)S(1)}, f32[768]{0:T(1024)}, u32[]{:S(2)}) copy-start(f32[768]{0:T(1024)} %param.58) | copy-start | bytes 9220
  397.6 25.1 %copy-start.145 = (f32[768]{0:T(1024)S(1)}, f32[768]{0:T(1024)}, u32[]{:S(2)}) copy-start(f32[768]{0:T(1024)} %param.59) | copy-start | bytes 9220
  398.5 25.6 %copy-start.102 = (f32[196,2]{0,1:T(2,128)}, f32[196,2]{0,1:T(2,128)S(1)}, u32[]{:S(2)}) copy-start(f32[196,2]{0,1:T(2,128)S(1)} %copy.274) | copy-start | bytes 4708
  398.7 25.5 %copy-start.49 = (f32[196,2]{1,0:T(8,128)}, f32[196,2]{1,0:T(8,128)S(1)}, u32[]{:S(2)}) copy-start(f32[196,2]{1,0:T(8,128)S(1)} %copy.275) | copy-start | bytes 4708
  400.8 27.6 %copy-start.76 = (bf16[768,192]{0,1:T(8,128)(2,1)S(1)}, bf16[768,192]{0,1:T(8,128)(2,1)}, u32[]{:S(2)}) copy-start(bf16[768,192]{0,1:T(8,128)(2,1)} %param.61) | copy-start | bytes 884740
  424.9 11.6 all-to-all-start
  436.5 11.6 all-to-all-start.1
  439.9 121.8 %all-reduce.24.cloned.1.call-start = ((), (), s32[]{:S(2)}) async-start(), calls=%async_computation.13 | async-start | bytes 9633792
  468.6 99.0 %copy-start.90 = (f32[768]{0:T(1024)S(1)}, f32[768]{0:T(1024)}, u32[]{:S(2)}) copy-start(f32[768]{0:T(1024)} %param.64) | copy-start | bytes 9220
  468.6 99.0 %copy-start.120 = (f32[768]{0:T(1024)S(1)}, f32[768]{0:T(1024)}, u32[]{:S(2)}) copy-start(f32[768]{0:T(1024)} %param.65) | copy-start | bytes 9220
  468.6 133.4 %all-gather.11.cloned.1.call-start = ((), (), s32[]{:S(2)}) async-start(), calls=%async_computation.7 | async-start | bytes 3010560 | tf_op jit(solution)/shard_map/all_gather | solution.py:34
  570.7 205.0 %copy-start.5 = (f32[196,2,768]{2,1,0:T(2,128)}, f32[196,2,768]{2,1,0:T(2,128)S(1)}, u32[]{:S(2)}) copy-start(f32[196,2,768]{2,1,0:T(2,128)S(1)} %get-tuple-element.779) | copy-start | bytes 3612676
  573.9 34.9 %copy-start.106 = (f32[196,2]{0,1:T(2,128)}, f32[196,2]{0,1:T(2,128)S(1)}, u32[]{:S(2)}) copy-start(f32[196,2]{0,1:T(2,128)S(1)} %copy.288) | copy-start | bytes 4708
  577.4 58.3 %all-gather.13.cloned.1.call-start = ((), (), s32[]{:S(2)}) async-start(), calls=%async_computation.8 | async-start | bytes 3010560 | tf_op jit(solution)/shard_map/all_gather | solution.py:34
  577.9 193.4 %all-reduce.26.cloned.1.call-start = ((), (), s32[]{:S(2)}) async-start(), calls=%async_computation.14 | async-start | bytes 9633792
  608.8 14.7 copy-start.11
  635.7 338.9 %copy-start.94 = (f32[784,2]{0,1:T(2,128)}, f32[784,2]{0,1:T(2,128)S(1)}, u32[]{:S(2)}) copy-start(f32[784,2]{0,1:T(2,128)S(1)} %get-tuple-element.808) | copy-start | bytes 18820
  673.9 97.4 %copy-start.39 = (f32[196,2]{1,0:T(8,128)S(1)}, f32[196,2]{1,0:T(8,128)}, u32[]{:S(2)}) copy-start(f32[196,2]{1,0:T(8,128)} %copy-done.38) | copy-start | bytes 4708
  673.9 97.4 %copy-start.51 = (f32[196,2]{1,0:T(8,128)S(1)}, f32[196,2]{1,0:T(8,128)}, u32[]{:S(2)}) copy-start(f32[196,2]{1,0:T(8,128)} %copy.289) | copy-start | bytes 4708
  673.9 101.7 %copy-start.107 = (f32[196,2]{0,1:T(2,128)S(1)}, f32[196,2]{0,1:T(2,128)}, u32[]{:S(2)}) copy-start(f32[196,2]{0,1:T(2,128)} %copy-done.106) | copy-start | bytes 4708
  673.9 140.6 %all-gather.15.cloned.1.call-start = ((), (), s32[]{:S(2)}) async-start(), calls=%async_computation.9 | async-start | bytes 3010560 | tf_op jit(solution)/shard_map/all_gather | solution.py:34
  784.9 29.6 %copy-start.70 = (bf16[192,768]{1,0:T(8,128)(2,1)S(1)}, bf16[192,768]{1,0:T(8,128)(2,1)}, u32[]{:S(2)}) copy-start(bf16[192,768]{1,0:T(8,128)(2,1)} %param.63) | copy-start | bytes 884740
  789.8 148.1 %all-reduce.28.cloned.1.call-start = ((), (), s32[]{:S(2)}) async-start(), calls=%async_computation.15 | async-start | bytes 9633792
  818.1 17.2 %copy-start.71 = (bf16[768,192]{0,1:T(8,128)(2,1)S(1)}, bf16[768,192]{0,1:T(8,128)(2,1)}, u32[]{:S(2)}) copy-start(bf16[768,192]{0,1:T(8,128)(2,1)} %param.60) | copy-start | bytes 884740
  842.1 95.8 %copy-start.8 = (f32[196,2,768]{2,1,0:T(2,128)S(1)}, f32[196,2,768]{2,1,0:T(2,128)}, u32[]{:S(2)}) copy-start(f32[196,2,768]{2,1,0:T(2,128)} %copy-done.7) | copy-start | bytes 3612676
  842.1 95.8 %copy-start.37 = (f32[196,2]{1,0:T(8,128)S(1)}, f32[196,2]{1,0:T(8,128)}, u32[]{:S(2)}) copy-start(f32[196,2]{1,0:T(8,128)} %copy-done.36) | copy-start | bytes 4708
  842.2 95.8 %copy-start.50 = (f32[196,2]{1,0:T(8,128)S(1)}, f32[196,2]{1,0:T(8,128)}, u32[]{:S(2)}) copy-start(f32[196,2]{1,0:T(8,128)} %copy-done.49) | copy-start | bytes 4708
  842.2 100.1 %copy-start.103 = (f32[196,2]{0,1:T(2,128)S(1)}, f32[196,2]{0,1:T(2,128)}, u32[]{:S(2)}) copy-start(f32[196,2]{0,1:T(2,128)} %copy-done.102) | copy-start | bytes 4708
  842.2 167.7 %all-gather.17.cloned.1.call-start = ((), (), s32[]{:S(2)}) async-start(), calls=%async_computation.10 | async-start | bytes 3010560 | tf_op jit(solution)/shard_map/all_gather | solution.py:34
  954.4 20.2 %copy-start.96 = (f32[784,2]{0,1:T(2,128)S(1)}, f32[784,2]{0,1:T(2,128)}, u32[]{:S(2)}) copy-start(f32[784,2]{0,1:T(2,128)} %get-tuple-element.809) | copy-start | bytes 18820
  954.4 20.2 %copy-start.121 = (f32[768]{0:T(1024)S(1)}, f32[768]{0:T(1024)}, u32[]{:S(2)}) copy-start(f32[768]{0:T(1024)} %param.69) | copy-start | bytes 9220
  954.4 20.2 %copy-start.143 = (f32[768]{0:T(1024)S(1)}, f32[768]{0:T(1024)}, u32[]{:S(2)}) copy-start(f32[768]{0:T(1024)} %param.70) | copy-start | bytes 9220
  956.7 14.3 all-to-all-start.3
  971.0 15.3 all-to-all-start.2
  974.6 149.4 %reduce-scatter.4.cloned.1.call-start = ((), (), s32[]{:S(2)}) async-start(), calls=%async_computation.11 | async-start | bytes 1966080
  1009.8 394.5 %all-reduce.32.cloned.1.call-start = ((), (), s32[]{:S(2)}) async-start(), calls=%async_computation.17 | async-start | bytes 19267584
  1017.4 66.1 %copy-start.73 = (bf16[768,192]{0,1:T(8,128)(2,1)S(1)}, bf16[768,192]{0,1:T(8,128)(2,1)}, u32[]{:S(2)}) copy-start(bf16[768,192]{0,1:T(8,128)(2,1)} %param.49) | copy-start | bytes 884740
  1064.8 14.1 copy-start.25
  1094.5 491.4 %all-reduce.30.cloned.1.call-start = ((), (), s32[]{:S(2)}) async-start(), calls=%async_computation.16 | async-start | bytes 18874368 | tf_op jit(solution)/shard_map/psum | solution.py:395
  1354.7 49.6 %copy-start.41 = (f32[196,2]{1,0:T(8,128)S(1)}, f32[196,2]{1,0:T(8,128)}, u32[]{:S(2)}) copy-start(f32[196,2]{1,0:T(8,128)} %copy-done.40) | copy-start | bytes 4708
  1354.7 49.6 %copy-start.53 = (f32[196,2]{1,0:T(8,128)S(1)}, f32[196,2]{1,0:T(8,128)}, u32[]{:S(2)}) copy-start(f32[196,2]{1,0:T(8,128)} %copy-done.52) | copy-start | bytes 4708
  1354.7 49.6 %copy-start.93 = (f32[768]{0:T(1024)S(1)}, f32[768]{0:T(1024)}, u32[]{:S(2)}) copy-start(f32[768]{0:T(1024)} %param.46) | copy-start | bytes 9220
  1361.1 43.2 %copy-start.10 = (bf16[196,2,768]{2,1,0:T(2,128)(2,1)S(1)}, bf16[196,2,768]{2,1,0:T(2,128)(2,1)}, u32[]{:S(2)}) copy-start(bf16[196,2,768]{2,1,0:T(2,128)(2,1)} %param.40) | copy-start | bytes 1806340
  1361.1 46.9 %copy-start.101 = (f32[196,2]{0,1:T(2,128)S(1)}, f32[196,2]{0,1:T(2,128)}, u32[]{:S(2)}) copy-start(f32[196,2]{0,1:T(2,128)} %copy-done.100) | copy-start | bytes 4708
  1361.2 47.1 %copy-start.108 = (f32[768]{0:T(1024)S(1)}, f32[768]{0:T(1024)}, u32[]{:S(2)}) copy-start(f32[768]{0:T(1024)} %get-tuple-element.614) | copy-start | bytes 9220
  1361.2 47.1 %copy-start.109 = (f32[768]{0:T(1024)S(1)}, f32[768]{0:T(1024)}, u32[]{:S(2)}) copy-start(f32[768]{0:T(1024)} %get-tuple-element.626) | copy-start | bytes 9220
  1361.2 47.1 %copy-start.110 = (f32[768]{0:T(1024)S(1)}, f32[768]{0:T(1024)}, u32[]{:S(2)}) copy-start(f32[768]{0:T(1024)} %get-tuple-element.616) | copy-start | bytes 9220
  1361.2 47.1 %copy-start.111 = (f32[768]{0:T(1024)S(1)}, f32[768]{0:T(1024)}, u32[]{:S(2)}) copy-start(f32[768]{0:T(1024)} %get-tuple-element.634) | copy-start | bytes 9220
  1361.2 47.1 %copy-start.112 = (f32[768]{0:T(1024)S(1)}, f32[768]{0:T(1024)}, u32[]{:S(2)}) copy-start(f32[768]{0:T(1024)} %get-tuple-element.618) | copy-start | bytes 9220
  1361.2 47.1 %copy-start.113 = (f32[768]{0:T(1024)S(1)}, f32[768]{0:T(1024)}, u32[]{:S(2)}) copy-start(f32[768]{0:T(1024)} %get-tuple-element.627) | copy-start | bytes 9220
  1361.2 47.1 %copy-start.114 = (f32[768]{0:T(1024)S(1)}, f32[768]{0:T(1024)}, u32[]{:S(2)}) copy-start(f32[768]{0:T(1024)} %get-tuple-element.620) | copy-start | bytes 9220
  1361.2 47.0 %copy-start.115 = (f32[768]{0:T(1024)S(1)}, f32[768]{0:T(1024)}, u32[]{:S(2)}) copy-start(f32[768]{0:T(1024)} %get-tuple-element.635) | copy-start | bytes 9220
  1403.3 48.3 %copy-start.128 = (f32[192]{0:T(256)}, f32[192]{0:T(256)S(1)}, u32[]{:S(2)}) copy-start(f32[192]{0:T(256)S(1)} %get-tuple-element.1424) | copy-start | bytes 2308
  1403.3 48.3 %copy-start.130 = (f32[192]{0:T(256)}, f32[192]{0:T(256)S(1)}, u32[]{:S(2)}) copy-start(f32[192]{0:T(256)S(1)} %get-tuple-element.1425) | copy-start | bytes 2308
  1408.0 43.7 %copy-start.6 = (f32[196,2,768]{2,1,0:T(2,128)S(1)}, f32[196,2,768]{2,1,0:T(2,128)}, u32[]{:S(2)}) copy-start(f32[196,2,768]{2,1,0:T(2,128)} %copy-done.5) | copy-start | bytes 3612676
  (110 other events, 466.0 us)
Sparse Core Ops, SparseCore 0:
  14.5 27.0 all-gather.6
  291.1 98.1 all-reduce.21
  400.6 24.5 all-gather.8
  468.7 93.0 all-reduce.23
  577.5 24.5 all-gather.10
  603.4 24.3 all-gather.12
  674.0 97.2 all-reduce.25
  790.0 24.5 all-gather.14
  842.3 95.5 all-reduce.27
  956.0 24.5 all-gather.16
  1009.9 29.1 reduce-scatter.3
  1094.6 174.3 all-reduce.31
  1278.6 307.2 all-reduce.29
where the time goes:
time: 1630 us; the launch traced here: 1610 us
  waiting for transfers between devices  585 us (36%)
  local copies, waits for them, and re-layouts  579 us (36%)
  other arithmetic  141 us (9%)
  matrix products  126 us (8%)
  blocking collectives  124 us (8%)
  loops' own time  17 us (1%)
  between operations  17 us (1%)
  starting transfers between devices  16.7 us (1%)
    unnamed x19, waiting for transfers between devices  383 us
    unnamed x302, local copies, waits for them, and re-layouts  275 us
    psum x1, waiting for transfers between devices, on_device(): lax.psum((grad_query, grad_key, grad_value, grad_table, grad_scale, grad_...  130 us
    rev x1, local copies, waits for them, and re-layouts, offset_sums(): flipped = jnp.flip(grad_bias, -1)  72.6 us
    all_gather x6, waiting for transfers between devices, spread_rows(): return lax.all_gather(shard, 'mp', axis=0, tiled=True)  48.7 us
    psum x1, blocking collectives, on_device(): lax.psum((grad_query, grad_key, grad_value, grad_table, grad_scale, grad_...  40.1 us
    psum x1, blocking collectives, on_device(): lax.psum((grad_self_gain, grad_self_bias, grad_after_gain, grad_after_bia...  40 us
  transfers between devices with their start and end apart: 17, of which 10 were waited for; matrix products, arithmetic and copies ran while one was open for 40% of the time, Pallas kernels for 0%

commit v1 on v0

v1 whole, which is shorter than its diff:
```python
import jax
import jax.numpy as jnp
from jax import lax
from jax.experimental import pallas as pl
from jax.experimental.pallas import tpu as pltpu
from jax.sharding import PartitionSpec as P

HEAD_DIM = 64
EPSILON = 1e-05
MASKED = -1e30
LANES = 128
BF = jnp.bfloat16
F32 = jnp.float32
SCALE = HEAD_DIM ** (-0.5)
VMEM_LIMIT = 50 * 1024 * 1024


def contract(left, right, left_dim, right_dim, precision=None):
    return lax.dot_general(
        left,
        right,
        (((left_dim,), (right_dim,)), ((), ())),
        precision=precision,
        preferred_element_type=F32,
    )


def kernel_params():
    return pltpu.CompilerParams(vmem_limit_bytes=VMEM_LIMIT)


def choice_of(ids, buckets):
    places = lax.broadcasted_iota(jnp.int32, (buckets, ids.shape[1]), 0)
    return jnp.where(places == ids, 1.0, 0.0).astype(F32)


def bias_kernel(ids_ref, table_ref, ext_ref):
    heads, width = 2 * ext_ref.shape[0], ext_ref.shape[2]
    choose = choice_of(ids_ref[...], table_ref.shape[1])
    by_offset = contract(table_ref[...], choose, 1, 0, lax.Precision.HIGHEST)
    sub = lax.broadcasted_iota(jnp.int32, (8, width), 0)
    for head in range(heads):
        rolled = jnp.broadcast_to(by_offset[head : head + 1, :], (8, width))
        for bit in (1, 2, 4):
            rolled = jnp.where((sub & bit) > 0, pltpu.roll(rolled, bit, 1), rolled)
        for group in range(LANES // 8):
            start = (head % 2) * LANES + group * 8
            moved = rolled if group == 0 else pltpu.roll(rolled, group * 8, 1)
            ext_ref[head // 2, start : start + 8, :] = moved


def halves(block, low):
    zero = jnp.zeros_like(block)
    return jnp.concatenate([jnp.where(low, block, zero), jnp.where(low, zero, block)], 0)


def merge(block, low):
    rows = block.shape[0] // 2
    return jnp.where(low, block[:rows], block[rows:])


def pair_columns(pair, base=0):
    return pl.ds(pl.multiple_of(base + pair * LANES, LANES), LANES)


def penalty_of(rows, first_row, count, seg_col, seg_row):
    i = lax.broadcasted_iota(jnp.int32, (rows, count), 0) + first_row
    j = lax.broadcasted_iota(jnp.int32, (rows, count), 1)
    one = jnp.where((j <= i) & (seg_col == seg_row), 0.0, MASKED).astype(F32)
    return jnp.concatenate([one, one], 0)


def ext_block(ext_ref, pair, rows, shift, count):
    if rows == LANES:
        return ext_ref[pair, :, shift : shift + count]
    return jnp.concatenate(
        [
            ext_ref[pair, 0:rows, shift : shift + count],
            ext_ref[pair, LANES : LANES + rows, shift : shift + count],
        ],
        0,
    )


def self_forward_kernel(qkv_ref, ext_ref, seg_col_ref, seg_row_ref, scale_ref, out_ref, stats_ref):
    length, width = out_ref.shape
    pairs = width // LANES
    blocks = -(-length // LANES)
    lane = lax.broadcasted_iota(jnp.int32, (1, LANES), 1)
    low = lane < HEAD_DIM
    stats_ref[...] = jnp.zeros_like(stats_ref)
    for block in range(blocks):
        start = block * LANES
        rows = min(LANES, length - start)
        count = start + rows
        shift = (blocks - 1 - block) * LANES
        penalty = penalty_of(
            rows, start, count, seg_col_ref[start : start + rows, :], seg_row_ref[:, 0:count]
        )

        def one_pair(pair, carry):
            columns = pair_columns(pair)
            query = halves(qkv_ref[start : start + rows, columns].astype(F32) * SCALE, low).astype(BF)
            key = qkv_ref[0:count, pair_columns(pair, width)]
            value = qkv_ref[0:count, pair_columns(pair, 2 * width)]
            scores = contract(query, key, 1, 1) + (
                ext_block(ext_ref, pair, rows, shift, count) + penalty
            )
            peak = jnp.max(scores, -1, keepdims=True)
            shifted = jnp.exp(scores - peak)
            total = jnp.sum(shifted, -1, keepdims=True)
            weights = (shifted * (1.0 / total)).astype(BF)
            mixed = merge(contract(weights, value, 1, 0), low)
            out_ref[start : start + rows, columns] = (mixed * scale_ref[:, columns]).astype(BF)
            level = peak + jnp.log(total)
            stats_ref[start : start + rows, :] += jnp.where(
                lane == 2 * pair, level[:rows], 0.0
            ) + jnp.where(lane == 2 * pair + 1, level[rows:], 0.0)
            return carry

        lax.fori_loop(0, pairs, one_pair, 0)


def level_of(stats, lane, pair):
    return jnp.concatenate(
        [
            jnp.sum(jnp.where(lane == 2 * pair + side, stats, 0.0), -1, keepdims=True)
            for side in (0, 1)
        ],
        0,
    )


def self_backward_kernel(
    qkv_ref,
    upstream_ref,
    ext_ref,
    seg_col_ref,
    seg_row_ref,
    stats_ref,
    ids_ref,
    grad_ref,
    table_ref,
    head_ref,
    key_sum,
    value_sum,
    offset_sum,
):
    length, width = upstream_ref.shape
    pairs = width // LANES
    blocks = -(-length // LANES)
    lane = lax.broadcasted_iota(jnp.int32, (1, LANES), 1)
    low = lane < HEAD_DIM
    key_sum[...] = jnp.zeros_like(key_sum)
    value_sum[...] = jnp.zeros_like(value_sum)
    offset_sum[...] = jnp.zeros_like(offset_sum)
    head_ref[...] = jnp.zeros_like(head_ref)
    for block in range(blocks):
        start = block * LANES
        rows = min(LANES, length - start)
        count = start + rows
        shift = (blocks - 1 - block) * LANES
        penalty = penalty_of(
            rows, start, count, seg_col_ref[start : start + rows, :], seg_row_ref[:, 0:count]
        )

        def one_pair(pair, carry):
            columns = pair_columns(pair)
            query = halves(qkv_ref[start : start + rows, columns].astype(F32) * SCALE, low).astype(BF)
            key = qkv_ref[0:count, pair_columns(pair, width)]
            value = qkv_ref[0:count, pair_columns(pair, 2 * width)]
            upstream = halves(upstream_ref[start : start + rows, columns].astype(F32), low).astype(BF)
            level = level_of(stats_ref[start : start + rows, :], lane, pair)
            scores = contract(query, key, 1, 1) + (
                ext_block(ext_ref, pair, rows, shift, count) + penalty
            )
            probs = jnp.exp(scores - level)
            grad_probs = contract(upstream, value, 1, 1)
            inner = jnp.sum(probs * grad_probs, -1, keepdims=True)
            grad_scores = (probs * (grad_probs - inner)).astype(BF)
            weights = probs.astype(BF)
            grad_query = merge(contract(grad_scores, key, 1, 0), low) * SCALE
            grad_ref[start : start + rows, columns] = grad_query.astype(BF)
            key_sum[0:count, columns] += contract(grad_scores, query, 0, 0)
            value_sum[0:count, columns] += contract(weights, upstream, 0, 0)
            wide = grad_scores.astype(F32)
            if rows == LANES:
                offset_sum[pair, :, shift : shift + count] += wide
            else:
                offset_sum[pair, 0:rows, shift : shift + count] += wide[:rows]
                offset_sum[pair, LANES : LANES + rows, shift : shift + count] += wide[rows:]
            for side in (0, 1):
                part = jnp.sum(inner[side * rows : (side + 1) * rows], 0, keepdims=True)
                head_ref[pl.ds(2 * pair + side, 1), :] += jnp.broadcast_to(part, (1, LANES))
            return carry

        lax.fori_loop(0, pairs, one_pair, 0)
    grad_ref[:, width : 2 * width] = key_sum[...].astype(BF)
    grad_ref[:, 2 * width : 3 * width] = value_sum[...].astype(BF)
    span = offset_sum.shape[2]
    sub = lax.broadcasted_iota(jnp.int32, (8, span), 0)
    head_places = lax.broadcasted_iota(jnp.int32, (table_ref.shape[0], span), 0)
    by_offset = jnp.zeros((table_ref.shape[0], span), F32)
    for head in range(2 * pairs):
        total = None
        for group in range(LANES // 8):
            first = (head % 2) * LANES + group * 8
            piece = offset_sum[head // 2, first : first + 8, :]
            moved = piece if group == 0 else pltpu.roll(piece, span - group * 8, 1)
            total = moved if total is None else total + moved
        for bit in (1, 2, 4):
            total = jnp.where((sub & bit) > 0, pltpu.roll(total, span - bit, 1), total)
        line = jnp.sum(total, 0, keepdims=True)
        by_offset = by_offset + jnp.where(head_places == head, line, 0.0)
    choose = choice_of(ids_ref[...], table_ref.shape[1])
    table_ref[...] = contract(by_offset, choose, 1, 1, lax.Precision.HIGHEST)


def cross_forward_kernel(query_ref, key_ref, value_ref, valid_ref, out_ref, stats_ref):
    pairs = query_ref.shape[1] // LANES
    lane = lax.broadcasted_iota(jnp.int32, (1, LANES), 1)
    low = lane < HEAD_DIM
    penalty = jnp.where(valid_ref[...] > 0, 0.0, MASKED).astype(F32)
    stats_ref[...] = jnp.zeros_like(stats_ref)

    def one_pair(pair, carry):
        columns = pair_columns(pair)
        query = query_ref[:, columns].astype(F32) * SCALE
        key = key_ref[:, columns]
        value = value_ref[:, columns]
        mixed = None
        for side in (0, 1):
            mine = low if side == 0 else jnp.logical_not(low)
            scores = contract(jnp.where(mine, query, 0.0).astype(BF), key, 1, 1) + penalty
            peak = jnp.max(scores, -1, keepdims=True)
            shifted = jnp.exp(scores - peak)
            total = jnp.sum(shifted, -1, keepdims=True)
            weights = (shifted * (1.0 / total)).astype(BF)
            part = contract(weights, value, 1, 0)
            mixed = part if mixed is None else jnp.where(low, mixed, part)
            stats_ref[...] += jnp.where(lane == 2 * pair + side, peak + jnp.log(total), 0.0)
        out_ref[:, columns] = mixed.astype(BF)
        return carry

    lax.fori_loop(0, pairs, one_pair, 0)


def cross_backward_kernel(
    query_ref,
    key_ref,
    value_ref,
    valid_ref,
    stats_ref,
    upstream_ref,
    grad_query_ref,
    grad_key_ref,
    grad_value_ref,
):
    pairs = query_ref.shape[1] // LANES
    lane = lax.broadcasted_iota(jnp.int32, (1, LANES), 1)
    low = lane < HEAD_DIM
    penalty = jnp.where(valid_ref[...] > 0, 0.0, MASKED).astype(F32)

    def one_pair(pair, carry):
        columns = pair_columns(pair)
        query = query_ref[:, columns].astype(F32) * SCALE
        upstream = upstream_ref[:, columns].astype(F32)
        key = key_ref[:, columns]
        value = value_ref[:, columns]
        grad_query = grad_key = grad_value = None
        for side in (0, 1):
            mine = low if side == 0 else jnp.logical_not(low)
            my_query = jnp.where(mine, query, 0.0).astype(BF)
            my_upstream = jnp.where(mine, upstream, 0.0).astype(BF)
            level = jnp.sum(
                jnp.where(lane == 2 * pair + side, stats_ref[...], 0.0), -1, keepdims=True
            )
            probs = jnp.exp(contract(my_query, key, 1, 1) + penalty - level)
            grad_probs = contract(my_upstream, value, 1, 1)
            inner = jnp.sum(probs * grad_probs, -1, keepdims=True)
            grad_scores = (probs * (grad_probs - inner)).astype(BF)
            part_query = contract(grad_scores, key, 1, 0)
            part_key = contract(grad_scores, my_query, 0, 0)
            part_value = contract(probs.astype(BF), my_upstream, 0, 0)
            if side == 0:
                grad_query, grad_key, grad_value = part_query, part_key, part_value
            else:
                grad_query = jnp.where(low, grad_query, part_query)
                grad_key, grad_value = grad_key + part_key, grad_value + part_value
        grad_query_ref[:, columns] = (grad_query * SCALE).astype(BF)
        grad_key_ref[:, columns] = grad_key
        grad_value_ref[:, columns] = grad_value
        return carry

    lax.fori_loop(0, pairs, one_pair, 0)


def flip_over(axis, bit):
    def send(block):
        size = lax.axis_size(axis)
        return lax.ppermute(block, axis, [(i, i ^ bit) for i in range(size)])

    return send


def mate(block):
    return flip_over("mp", 1)(block)


def peer(block):
    return flip_over("mp", 2)(block)


def in_order(index, own, other, axis=0):
    first = jnp.where(index == 0, own, other)
    second = jnp.where(index == 0, other, own)
    return jnp.concatenate([first, second], axis)


def cut(block, index, size, axis=0):
    return lax.dynamic_slice_in_dim(block, index * size, size, axis)


def dot(left, right):
    return jnp.dot(left, right, preferred_element_type=F32)


def dot_right(left, right):
    return contract(left, right, 1, 1)


def dot_left(left, right):
    return contract(left, right, 0, 0)


def norm_parts(values):
    center = values - jnp.mean(values, -1, keepdims=True)
    factor = lax.rsqrt(jnp.mean(center * center, -1, keepdims=True) + EPSILON)
    return center * factor, factor


def norm_back(values, gain, upstream):
    hat, factor = norm_parts(values)
    leaned = upstream * gain
    grad = factor * (
        leaned
        - jnp.mean(leaned, -1, keepdims=True)
        - hat * jnp.mean(leaned * hat, -1, keepdims=True)
    )
    return grad, jnp.sum(upstream * hat, 0), jnp.sum(upstream, 0)


def batch_bits():
    size = lax.axis_size("batch")
    bits = []
    while (1 << len(bits)) < size:
        bits.append(1 << len(bits))
    return bits


def sum_rows(block, axis_bits):
    for axis, bit in axis_bits:
        index = (lax.axis_index(axis) // bit) % 2
        size = block.shape[0] // 2
        keep = cut(block, index, size)
        send = cut(block, 1 - index, size).astype(BF)
        block = keep + flip_over(axis, bit)(send).astype(F32)
    block = block.astype(BF)
    for axis, bit in reversed(axis_bits):
        index = (lax.axis_index(axis) // bit) % 2
        block = in_order(index, block, flip_over(axis, bit)(block))
    return block.astype(F32)


def sum_small(block, axis_bits):
    for axis, bit in axis_bits:
        block = block + flip_over(axis, bit)(block)
    return block


def pack_small(parts):
    flat = jnp.concatenate([part.reshape(-1) for part in parts])
    size = -(-flat.shape[0] // (8 * LANES)) * 8 * LANES
    return jnp.pad(flat, (0, size - flat.shape[0])).reshape(-1, LANES)


def unpack_small(packed, shapes):
    flat = packed.reshape(-1)
    parts, start = [], 0
    for shape in shapes:
        size = 1
        for extent in shape:
            size *= extent
        parts.append(flat[start : start + size].reshape(shape))
        start += size
    return parts


def shape_of(shape, dtype):
    return jax.ShapeDtypeStruct(shape, dtype)


def on_device(
    tokens,
    segment_ids,
    bucket_ids,
    memory,
    memory_mask,
    cotangent,
    self_gain,
    self_bias,
    query_weight,
    key_weight,
    value_weight,
    rel_table,
    head_scale,
    output_weight,
    after_gain,
    after_bias,
    cross_gain,
    cross_bias,
    batch_gain,
    batch_bias,
    cross_query,
    cross_key,
    cross_value,
    cross_output,
    crossout_gain,
    crossout_bias,
    ffn_gain,
    ffn_bias,
    up_weight,
    middle_gain,
    middle_bias,
    down_weight,
):
    place = lax.axis_index("mp")
    core, side = place % 2, place // 2
    batch = lax.axis_size("batch")
    bits = batch_bits()
    over_batch = [("batch", bit) for bit in bits]
    quarter, _, width = tokens.shape
    length = 4 * quarter
    half = 2 * quarter
    heads = 2 * rel_table.shape[1]
    lanes = heads * HEAD_DIM
    own_lanes = lanes // 2
    hidden = 2 * up_weight.shape[1]
    all_hidden = 2 * hidden

    def own_row(array):
        keep = lax.dynamic_index_in_dim(array, core, 1, keepdims=False)
        give = lax.dynamic_index_in_dim(array, 1 - core, 1, keepdims=False)
        near = mate(give)
        far = peer(keep)
        cross = flip_over("mp", 3)(give)
        return in_order(core, keep, near), in_order(core, far, cross)

    own_tokens, far_tokens = own_row(tokens)
    row_tokens = in_order(side, own_tokens, far_tokens).astype(F32)
    stream = own_tokens.astype(F32)

    rows_here = memory.reshape(memory.shape[0], batch, 2, width)
    my_rows = lax.dynamic_index_in_dim(rows_here, core, 2, keepdims=False)
    row_memory = lax.all_to_all(my_rows, "batch", split_axis=1, concat_axis=0, tiled=True)
    row_memory = row_memory.reshape(-1, width)
    mem_float = memory.astype(F32)
    mem_totals = sum_small(
        pack_small([jnp.sum(mem_float, (0, 1)), jnp.sum(mem_float * mem_float, (0, 1))]), over_batch
    )
    mem_sum, mem_square = unpack_small(mem_totals, [(width,), (width,)])

    blocks = -(-length // LANES)
    span = blocks * LANES
    split = length - 1 - (blocks - 1) * LANES
    ids = jnp.concatenate(
        [
            bucket_ids[split:length],
            jnp.full((span - length,), -1, bucket_ids.dtype),
            bucket_ids[:split],
        ]
    )[None, :]
    table = jnp.concatenate([rel_table, mate(rel_table)], 1).T
    table = jnp.pad(table, ((0, 8 - heads % 8), (0, 0)))
    ext = pl.pallas_call(
        bias_kernel,
        out_shape=shape_of((heads // 2, 2 * LANES, span), F32),
        compiler_params=kernel_params(),
        name="bias",
    )(ids, table)

    near_weights = mate(jnp.stack([query_weight, key_weight, value_weight]))
    qkv_weight = jnp.concatenate(
        [
            query_weight,
            near_weights[0],
            key_weight,
            near_weights[1],
            value_weight,
            near_weights[2],
        ],
        1,
    )
    token_hat, _ = norm_parts(row_tokens)
    self_in = (token_hat * self_gain + self_bias).astype(BF)
    qkv = dot(self_in, qkv_weight).astype(BF)
    segment = lax.dynamic_index_in_dim(segment_ids, core, 0, keepdims=False)
    seg_col, seg_row = segment[:, None], segment[None, :]
    both_scale = jnp.concatenate([head_scale, mate(head_scale)])
    scale_lanes = jnp.repeat(both_scale, HEAD_DIM)[None, :]
    scaled, stats = pl.pallas_call(
        self_forward_kernel,
        out_shape=(shape_of((length, lanes), BF), shape_of((length, LANES), F32)),
        compiler_params=kernel_params(),
        name="self_forward",
    )(qkv, ext, seg_col, seg_row, scale_lanes)
    own_scaled = jnp.concatenate([cut(scaled, side, half), peer(cut(scaled, 1 - side, half))], 1)

    def whole(weight, axis):
        near = mate(weight)
        far = peer(weight)
        return jnp.concatenate([weight, near, far, mate(far)], axis)

    output_all = whole(output_weight, 0)
    attn = dot(own_scaled, output_all)
    attn_hat, _ = norm_parts(attn)
    first = stream + attn_hat * after_gain + after_bias
    first_hat, _ = norm_parts(first)
    cross_in = (first_hat * cross_gain + cross_bias).astype(BF)
    cross_query_all = whole(cross_query, 1)
    cross_queries = dot(cross_in, cross_query_all).astype(BF)

    count = memory.shape[0] * batch * memory.shape[1]
    mem_mean = mem_sum / count
    mem_scale = lax.rsqrt(mem_square / count - mem_mean * mem_mean + EPSILON)
    normed = (((row_memory.astype(F32) - mem_mean) * mem_scale) * batch_gain + batch_bias).astype(BF)
    kv_weight = jnp.concatenate([cross_key, mate(cross_key), cross_value, mate(cross_value)], 1)
    own_kv = dot(normed, kv_weight).astype(BF)
    far_kv = peer(own_kv)
    mem_keys = jnp.concatenate([own_kv[:, :own_lanes * 2], far_kv[:, :own_lanes * 2]], 1)
    mem_values = jnp.concatenate([own_kv[:, own_lanes * 2 :], far_kv[:, own_lanes * 2 :]], 1)
    valid = lax.dynamic_index_in_dim(memory_mask, core, 0, keepdims=True)
    cross_mixed, cross_stats = pl.pallas_call(
        cross_forward_kernel,
        out_shape=(shape_of((half, width), BF), shape_of((half, LANES), F32)),
        compiler_params=kernel_params(),
        name="cross_forward",
    )(cross_queries, mem_keys, mem_values, valid)
    cross_output_all = whole(cross_output, 0)
    cross_attn = dot(cross_mixed, cross_output_all)
    cross_hat, _ = norm_parts(cross_attn)
    second = first + cross_hat * crossout_gain + crossout_bias
    second_hat, _ = norm_parts(second)
    ffn_own = (second_hat * ffn_gain + ffn_bias).astype(BF)

    ffn_in = jnp.concatenate([ffn_own, peer(ffn_own)], 0)
    own_cotangent, far_cotangent = own_row(cotangent)
    row_cotangent = jnp.concatenate([own_cotangent, far_cotangent], 0)
    up_pair = jnp.concatenate([up_weight, mate(up_weight)], 1)
    down_pair = jnp.concatenate([down_weight, mate(down_weight)], 0)
    near_middle = mate(jnp.stack([middle_gain, middle_bias]))
    gain_pair = jnp.concatenate([middle_gain, near_middle[0]])
    bias_pair = jnp.concatenate([middle_bias, near_middle[1]])
    gate = dot(ffn_in, up_pair)
    chance = 0.5 * (1.0 + lax.erf(gate * (0.5**0.5)))
    active = gate * chance
    grad_middle = dot_right(row_cotangent, down_pair)
    leaned = grad_middle * gain_pair
    sums = jnp.stack(
        [
            jnp.sum(active, -1),
            jnp.sum(active * active, -1),
            jnp.sum(leaned, -1),
            jnp.sum(leaned * active, -1),
        ]
    )
    far_sums = peer(sums)
    sums = sums + jnp.concatenate([far_sums[:, half:], far_sums[:, :half]], 1)
    sums = sums / all_hidden
    act_mean = sums[0][:, None]
    act_scale = lax.rsqrt(sums[1][:, None] - act_mean * act_mean + EPSILON)
    act_hat = (active - act_mean) * act_scale
    middle = (act_hat * gain_pair + bias_pair).astype(BF)
    leaned_mean = sums[2][:, None]
    leaned_hat = act_scale * (sums[3][:, None] - act_mean * leaned_mean)
    grad_active = act_scale * (leaned - leaned_mean - act_hat * leaned_hat)
    density = jnp.exp(-0.5 * gate * gate) * ((2.0 * jnp.pi) ** -0.5)
    grad_gate = (grad_active * (chance + gate * density)).astype(BF)
    grad_mid_gain = jnp.sum(grad_middle * act_hat, 0)
    grad_mid_bias = jnp.sum(grad_middle, 0)
    back_far = dot_right(grad_gate[half:], up_pair).astype(BF)
    back_came = peer(back_far)
    grad_ffn_in = dot_right(grad_gate[:half], up_pair) + back_came.astype(F32)

    back_second, grad_ffn_gain, grad_ffn_bias = norm_back(second, ffn_gain, grad_ffn_in)
    grad_second = own_cotangent.astype(F32) + back_second
    back_cross, grad_co_gain, grad_co_bias = norm_back(cross_attn, crossout_gain, grad_second)
    grad_cross_attn = back_cross.astype(BF)
    grad_cross_mixed = dot_right(grad_cross_attn, cross_output_all).astype(BF)
    grad_cq, grad_mk, grad_mv = pl.pallas_call(
        cross_backward_kernel,
        out_shape=(
            shape_of((half, width), BF),
            shape_of((row_memory.shape[0], width), F32),
            shape_of((row_memory.shape[0], width), F32),
        ),
        compiler_params=kernel_params(),
        name="cross_backward",
    )(cross_queries, mem_keys, mem_values, valid, cross_stats, grad_cross_mixed)
    grad_cross_in = dot_right(grad_cq, cross_query_all)
    back_first, grad_cross_gain, grad_cross_bias = norm_back(first, cross_gain, grad_cross_in)
    grad_first = grad_second + back_first
    back_attn, grad_after_gain, grad_after_bias = norm_back(attn, after_gain, grad_first)
    grad_attn = back_attn.astype(BF)
    all_scale = jnp.concatenate([both_scale, peer(both_scale)])
    grad_mixed_own = (
        dot_right(grad_attn, output_all) * jnp.repeat(all_scale, HEAD_DIM)[None, :]
    ).astype(BF)
    grad_mixed = in_order(side, grad_mixed_own[:, :lanes], peer(grad_mixed_own[:, lanes:]))
    grad_qkv, grad_table, grad_heads = pl.pallas_call(
        self_backward_kernel,
        out_shape=(
            shape_of((length, 3 * lanes), BF),
            shape_of(table.shape, F32),
            shape_of((8, LANES), F32),
        ),
        scratch_shapes=[
            pltpu.VMEM((length, lanes), F32),
            pltpu.VMEM((length, lanes), F32),
            pltpu.VMEM(ext.shape, F32),
        ],
        compiler_params=kernel_params(),
        name="self_backward",
    )(qkv, grad_mixed, ext, seg_col, seg_row, stats, ids)
    far_in = dot_right(cut(grad_qkv, 1 - side, half), qkv_weight).astype(BF)
    grad_self_in = dot_right(cut(grad_qkv, side, half), qkv_weight) + peer(far_in).astype(F32)
    back_tokens, grad_self_gain, grad_self_bias = norm_back(stream, self_gain, grad_self_in)
    own_grad_tokens = grad_first + back_tokens

    def by_quarter(own):
        keep = cut(own, core, quarter)
        came = mate(cut(own, 1 - core, quarter))
        return jnp.stack([jnp.where(core == 0, keep, came), jnp.where(core == 0, came, keep)], 1)

    grad_tokens = by_quarter(own_grad_tokens)
    out_far = dot(middle[half:], down_pair).astype(BF)
    out_own = second + dot(middle[:half], down_pair) + peer(out_far).astype(F32)
    output = by_quarter(out_own.astype(BF))

    def own_columns(grads):
        cols = width // 2
        return (grads[:, :cols] + peer(grads[:, cols:].astype(BF)).astype(F32)).astype(BF)

    grad_kv = jnp.concatenate([own_columns(grad_mk), own_columns(grad_mv)], 1)
    part_normed = dot_right(grad_kv, kv_weight)
    half_normed = cut(part_normed, side, width // 2, 1) + peer(
        cut(part_normed, 1 - side, width // 2, 1).astype(BF)
    ).astype(F32)
    channels = width // 4
    keep_normed = cut(half_normed, core, channels, 1)
    came_normed = mate(cut(half_normed, 1 - core, channels, 1))
    both_normed = jnp.stack(
        [
            jnp.where(core == 0, keep_normed, came_normed),
            jnp.where(core == 0, came_normed, keep_normed),
        ],
        1,
    )
    grad_normed = lax.all_to_all(both_normed, "batch", split_axis=0, concat_axis=1, tiled=True)
    mean_slice = cut(mem_mean, place, channels)
    gain_slice = cut(batch_gain, place, channels)
    scale_slice = cut(mem_scale, place, channels)
    hat_slice = (cut(memory, place, channels, 2).astype(F32) - mean_slice) * scale_slice
    shift_term = jnp.sum(grad_normed, (0, 1))
    scale_term = jnp.sum(grad_normed * hat_slice, (0, 1))

    def own_near(grads, axis):
        size = grads.shape[axis] // 2
        keep = lax.slice_in_dim(grads, 0, size, axis=axis)
        give = lax.slice_in_dim(grads, size, 2 * size, axis=axis)
        return keep + mate(give.astype(BF)).astype(F32)

    def own_of_four(grads, axis):
        size = grads.shape[axis] // 4
        part = [lax.slice_in_dim(grads, i * size, (i + 1) * size, axis=axis) for i in range(4)]
        came = mate(jnp.concatenate([part[1], part[3]], axis).astype(BF)).astype(F32)
        near = part[0] + lax.slice_in_dim(came, 0, size, axis=axis)
        far = part[2] + lax.slice_in_dim(came, size, 2 * size, axis=axis)
        return near + peer(far.astype(BF)).astype(F32)

    grad_up = own_near(dot_left(ffn_in, grad_gate), 1)
    grad_down = own_near(dot_left(middle, row_cotangent), 0)
    sum_ffn = sum_rows(jnp.concatenate([grad_up, grad_down], 0), over_batch)
    sum_up, sum_down = sum_ffn[: grad_up.shape[0]], sum_ffn[grad_up.shape[0] :]
    sum_coutput = sum_rows(own_of_four(dot_left(cross_mixed, grad_cross_attn), 0), over_batch)
    grad_cquery = own_of_four(dot_left(cross_in, grad_cq), 1)
    grad_ckv = dot_left(normed, grad_kv)
    cols = width // 2
    grad_ckey = own_near(grad_ckv[:, :cols], 1)
    grad_cvalue = own_near(grad_ckv[:, cols:], 1)
    sum_cross = sum_rows(jnp.concatenate([grad_cquery, grad_ckey, grad_cvalue], 1), over_batch)
    sum_output = sum_rows(own_of_four(dot_left(own_scaled, grad_attn), 0), over_batch)
    grad_weights = dot_left(self_in, grad_qkv)
    sum_qkv = sum_rows(
        jnp.concatenate(
            [own_near(grad_weights[:, i * lanes : (i + 1) * lanes], 1) for i in range(3)], 1
        ),
        over_batch,
    )
    step = width // 4

    own_heads = heads // 2
    mine_small = pack_small(
        [
            grad_table[:own_heads],
            grad_heads[:own_heads, 0] / both_scale[:own_heads],
            grad_mid_gain[: hidden // 2],
            grad_mid_bias[: hidden // 2],
        ]
    )
    near_small = pack_small(
        [
            grad_table[own_heads:heads],
            grad_heads[own_heads:heads, 0] / both_scale[own_heads:],
            grad_mid_gain[hidden // 2 :],
            grad_mid_bias[hidden // 2 :],
        ]
    )
    small = mine_small + mate(near_small)
    mem_small = pack_small([shift_term, scale_term])
    shared = sum_small(
        pack_small(
            [
                grad_self_gain,
                grad_self_bias,
                grad_after_gain,
                grad_after_bias,
                grad_cross_gain,
                grad_cross_bias,
                grad_co_gain,
                grad_co_bias,
                grad_ffn_gain,
                grad_ffn_bias,
            ]
        ),
        [("mp", 1), ("mp", 2)],
    )
    joined = sum_small(jnp.concatenate([small, mem_small, shared], 0), over_batch)
    a, b = small.shape[0], small.shape[0] + mem_small.shape[0]
    sum_table, sum_scale, sum_mid_gain, sum_mid_bias = unpack_small(
        joined[:a],
        [(own_heads, table.shape[1]), (own_heads,), (hidden // 2,), (hidden // 2,)],
    )
    shift_total, scale_total = unpack_small(joined[a:b], [(channels,), (channels,)])
    norm_totals = unpack_small(joined[b:], [(width,)] * 10)
    grad_memory = (
        gain_slice
        * scale_slice
        * (grad_normed - shift_total / count - hat_slice * scale_total / count)
    )
    return (
        output,
        grad_tokens,
        grad_memory,
        norm_totals[0],
        norm_totals[1],
        sum_qkv[:, :step],
        sum_qkv[:, step : 2 * step],
        sum_qkv[:, 2 * step :],
        sum_table.T,
        sum_scale,
        sum_output,
        norm_totals[2],
        norm_totals[3],
        norm_totals[4],
        norm_totals[5],
        scale_total,
        shift_total,
        sum_cross[:, :step],
        sum_cross[:, step : 2 * step],
        sum_cross[:, 2 * step :],
        sum_coutput,
        norm_totals[6],
        norm_totals[7],
        norm_totals[8],
        norm_totals[9],
        sum_up,
        sum_mid_gain,
        sum_mid_bias,
        sum_down,
    )


def solution(mesh):
    in_specs = (
        P("mp", "batch", None),
        P("batch", None),
        P(),
        P("batch", None, None),
        P("batch", None),
        P("mp", "batch", None),
        P(),
        P(),
        P(None, "mp"),
        P(None, "mp"),
        P(None, "mp"),
        P(None, "mp"),
        P("mp"),
        P("mp", None),
        P(),
        P(),
        P(),
        P(),
        P(),
        P(),
        P(None, "mp"),
        P(None, "mp"),
        P(None, "mp"),
        P("mp", None),
        P(),
        P(),
        P(),
        P(),
        P(None, "mp"),
        P("mp"),
        P("mp"),
        P("mp", None),
    )
    out_specs = (
        P("mp", "batch", None),
        P("mp", "batch", None),
        P("batch", None, "mp"),
        P(),
        P(),
        P(None, "mp"),
        P(None, "mp"),
        P(None, "mp"),
        P(None, "mp"),
        P("mp"),
        P("mp", None),
        P(),
        P(),
        P(),
        P(),
        P("mp"),
        P("mp"),
        P(None, "mp"),
        P(None, "mp"),
        P(None, "mp"),
        P("mp", None),
        P(),
        P(),
        P(),
        P(),
        P(None, "mp"),
        P("mp"),
        P("mp"),
        P("mp", None),
    )
    return jax.shard_map(
        on_device, mesh=mesh, in_specs=in_specs, out_specs=out_specs, check_vma=False
    )
```

time: 1630 us -> 515 us (0.32); the launches traced: 1610 us -> 509 us
  local copies, waits for them, and re-layouts: 579 us -> 69.2 us
  waiting for transfers between devices: 585 us -> 165 us
  blocking collectives: 124 us -> 0 us
  starting transfers between devices: 16.7 us -> 99.9 us
  matrix products: 126 us -> 44.6 us
  other arithmetic: 141 us -> 74.3 us
  Pallas kernels: 0 us -> 52.7 us
  loops' own time: 17 us -> 0 us
    unnamed x19 -> x0, waiting for transfers between devices: 383 us -> none
    unnamed x302 -> x271, local copies, waits for them, and re-layouts: 275 us -> 37.2 us
    ppermute x0 -> x90, waiting for transfers between devices: none -> 165 us  [send(): return lax.ppermute(block, axis, [(i, i ^ bit) for i in range(size)])]
    psum x1 -> x0, waiting for transfers between devices: 130 us -> none  [on_device(): lax.psum((grad_query, grad_key, grad_value, grad_table, grad_scale, grad_...]
    psum x5 -> x0, blocking collectives: 124 us -> none  [the longest x1 40.1 us: on_device(): lax.psum((grad_query, grad_key, grad_value, grad_table, grad_scale, grad_...]
    ppermute x0 -> x90, starting transfers between devices: none -> 88.2 us  [send(): return lax.ppermute(block, axis, [(i, i ^ bit) for i in range(size)])]
    reshape x4 -> x7, local copies, waits for them, and re-layouts: 87 us -> 0.63 us  [the longest x1 0.6 us: unpack_small(): parts.append(flat[start:start + size].reshape(shape))]
    dot_general x60 -> x24, matrix products: 126 us -> 44.6 us  [the longest x16 33.2 us: contract(): lax.dot_general(left, right, (((left_dim,), (right_dim,)), ((), ())), pre...]
  transfers between devices with their start and end apart: 17 -> 92, of which waited for: 10 -> 42; matrix products, arithmetic and copies ran while one was open for 40% -> 29% of each run, Pallas kernels for 0% -> 10%
where the time goes in v1:
time: 515 us; the launch traced here: 509 us
  waiting for transfers between devices  165 us (32%)
  starting transfers between devices  99.9 us (19%)
  other arithmetic  74.3 us (14%)
  local copies, waits for them, and re-layouts  69.2 us (13%)
  Pallas kernels  52.7 us (10%)
  matrix products  44.6 us (9%)
    ppermute x90, waiting for transfers between devices, send(): return lax.ppermute(block, axis, [(i, i ^ bit) for i in range(size)])  165 us
    ppermute x90, starting transfers between devices, send(): return lax.ppermute(block, axis, [(i, i ^ bit) for i in range(size)])  88.2 us
    unnamed x271, local copies, waits for them, and re-layouts  37.2 us
    dot_general x16, matrix products, contract(): lax.dot_general(left, right, (((left_dim,), (right_dim,)), ((), ())), pre...  33.2 us
    pallas_call x1, Pallas kernels, on_device(): pl.pallas_call(self_backward_kernel, out_shape=(shape_of((length, 3 * lan...  21.7 us
    pallas_call x1, Pallas kernels, on_device(): pl.pallas_call(self_forward_kernel, out_shape=(shape_of((length, lanes),...  16 us
    dot_general x8, matrix products, dot(): return jnp.dot(left, right, preferred_element_type=F32)  11.3 us
  transfers between devices with their start and end apart: 92, of which 42 were waited for; matrix products, arithmetic and copies ran while one was open for 29% of the time, Pallas kernels for 10%

profile of v1, /device:TPU:0, one launch (start us, length us, event | category | flops | bytes accessed | tf_op | source)
XLA Modules:
  0.0 509.3 jit_solution(13364260952810889604)
XLA Ops:
  0.7 4.9 constant_dynamic-slice_fusion.4
  6.9 2.6 collective-permute-start.2
  11.0 6.7 %all-to-all-start = ((bf16[32,8,768]{2,0,1:T(8,128)(2,1)}), bf16[32,8,768]{2,0,1:T(8,128)(2,1)}, u32[]{:S(2)}, u32[]{:S(2)}) async-start(bf16[32,8,768]{2,0,1:T(8,128)(2,1)} %dynamic-slice_bitcast_fusion), calls=%async_computation | async-start | bytes 786432 | tf_op jit(solution)/shard_map/all_to_all | solution.py:465
  23.6 2.4 constant_dynamic-update-slice_fusion.20
  26.7 2.4 constant_dynamic-update-slice_fusion.22
  46.0 3.0 collective-permute-start.15
  56.6 5.1 collective-permute-done.11
  63.9 6.2 %collective-permute-done.20 = bf16[192,768]{1,0:T(8,128)(2,1)S(1)} collective-permute-done((bf16[192,768]{1,0:T(8,128)(2,1)S(1)}, bf16[192,768]{1,0:T(8,128)(2,1)S(1)}, u32[]{:S(2)}, u32[]{:S(2)}) %collective-permute-start.20) | collective-permute-done | bytes 294944 | tf_op jit(solution)/shard_map/ppermute | solution.py:301
  76.6 7.7 %collective-permute-done.1 = bf16[196,768]{1,0:T(8,128)(2,1)S(1)} collective-permute-done((bf16[196,768]{1,0:T(8,128)(2,1)S(1)}, bf16[196,768]{1,0:T(8,128)(2,1)S(1)}, u32[]{:S(2)}, u32[]{:S(2)}) %collective-permute-start.1) | collective-permute-done | bytes 301088 | tf_op jit(solution)/shard_map/ppermute | solution.py:301
  95.9 16.0 %self_forward.1 = (bf16[784,384]{1,0:T(8,128)(2,1)S(1)}, f32[784,128]{1,0:T(8,128)S(1)}) custom-call(bf16[784,1152]{1,0:T(8,128)(2,1)S(1)} %convolution_convert_fusion.qkv_ref, f32[3,256,896]{2,1,0:T(8,128)} %copy-done.2, s32[784,1]{1,0:T(8,128)S(1)} %copy.124.seg_col_ref, s32[1,784]{1,0:T(1,128)S(1)} %constant_dynamic-slice_fusion.8.seg_row_ref, ...), custom_call_target="tpu_custom_call" | custom-call | tf_op jit(solution)/shard_map/self_forward/pallas_call | solution.py:511
  113.5 5.5 %collective-permute-done.6 = bf16[392,384]{1,0:T(8,128)(2,1)S(1)} collective-permute-done((bf16[392,384]{1,0:T(8,128)(2,1)S(1)}, bf16[392,384]{1,0:T(8,128)(2,1)S(1)}, u32[]{:S(2)}, u32[]{:S(2)}) %collective-permute-start.6) | collective-permute-done | bytes 301088 | tf_op jit(solution)/shard_map/ppermute | solution.py:301
  123.3 4.8 cross_forward.1
  137.2 4.2 collective-permute-done.22
  143.4 3.0 multiply_reduce_fusion.3
  147.6 2.8 collective-permute-done.29
  150.6 5.3 %fusion.85 = (f32[1536]{0:T(1024)S(1)}, f32[1536]{0:T(1024)S(1)}, bf16[784,1536]{1,0:T(8,128)(2,1)S(1)}, bf16[784,1536]{1,0:T(8,128)(2,1)S(1)}) fusion(f32[784,1536]{1,0:T(8,128)S(1)} %get-tuple-element.325, f32[784]{0:T(1024)S(1)} %get-tuple-element.319, f32[784,1536]{1,0:T(8,128)S(1)} %get-tuple-element.207, f32[784]{0:T(1024)S(1)} %get-tuple-element.196, ...), kind=kLoop, calls=%fused_computation.394 | loop fusion | flops 27694080 | bytes 19304704 | tf_op jit(solution)/shard_map/reduce_sum | solution.py:590
  155.9 2.7 fusion.57
  158.6 2.4 convolution_convert_fusion.2
  165.3 2.7 fusion.44
  172.4 8.4 %collective-permute-done.32 = bf16[392,768]{1,0:T(8,128)(2,1)S(1)} collective-permute-done((bf16[392,768]{1,0:T(8,128)(2,1)S(1)}, bf16[392,768]{1,0:T(8,128)(2,1)S(1)}, u32[]{:S(2)}, u32[]{:S(2)}) %collective-permute-start.32) | collective-permute-done | bytes 602144 | tf_op jit(solution)/shard_map/ppermute | solution.py:301
  184.0 2.2 fusion.111
  186.9 8.6 %cross_backward.1 = (bf16[392,768]{1,0:T(8,128)(2,1)S(1)}, f32[256,768]{1,0:T(8,128)S(1)}, f32[256,768]{1,0:T(8,128)}) custom-call(bf16[392,768]{1,0:T(8,128)(2,1)S(1)} %convolution_convert_fusion.5.query_ref, bf16[256,768]{1,0:T(8,128)(2,1)S(1)} %get-tuple-element.341.key_ref, bf16[256,768]{1,0:T(8,128)(2,1)S(1)} %get-tuple-element.342.value_ref, ...), custom_call_target="tpu_custom_call" | custom-call | tf_op jit(solution)/shard_map/cross_backward/pallas_call | solution.py:600
  195.6 2.4 fusion.110
  206.2 2.2 fusion.108
  220.0 2.7 collective-permute-done.34
  222.9 21.7 %self_backward.1 = (bf16[784,1152]{1,0:T(8,128)(2,1)S(1)}, f32[8,256]{1,0:T(8,128)S(1)}, f32[8,128]{1,0:T(8,128)S(1)}) custom-call(bf16[784,1152]{1,0:T(8,128)(2,1)} %copy-done.3, bf16[784,384]{1,0:T(8,128)(2,1)S(1)} %pad_maximum_fusion.14.upstream_ref, f32[3,256,896]{2,1,0:T(8,128)} %copy-done.2, s32[784,1]{1,0:T(8,128)S(1)} %copy.124.seg_col_ref, ...), custom_call_target="tpu_custom_call" | custom-call | tf_op jit(solution)/shard_map/self_backward/pallas_call | solution.py:620
  244.6 4.3 fusion.107
  250.5 3.3 convolution_convert_fusion.3
  256.4 2.4 copy.139
  260.0 6.0 %collective-permute-done.39 = bf16[256,384]{1,0:T(8,128)(2,1)S(1)} collective-permute-done((bf16[256,384]{1,0:T(8,128)(2,1)}, bf16[256,384]{1,0:T(8,128)(2,1)S(1)}, u32[]{:S(2)}, u32[]{:S(2)}) %collective-permute-start.39) | collective-permute-done | bytes 196640 | tf_op jit(solution)/shard_map/ppermute | solution.py:301
  268.0 2.8 slice_add_fusion.3
  273.7 2.8 slice_add_fusion.1
  281.0 2.3 fusion.46
  285.7 2.3 fusion.48
  291.5 5.0 all-to-all-start.1
  299.5 2.2 slice_add_fusion.8
  302.2 4.4 collective-permute-done.75
  309.9 5.2 %collective-permute-done.65 = bf16[768,192]{1,0:T(8,128)(2,1)S(1)} collective-permute-done((bf16[768,192]{1,0:T(8,128)(2,1)}, bf16[768,192]{1,0:T(8,128)(2,1)S(1)}, u32[]{:S(2)}, u32[]{:S(2)}) %collective-permute-start.65) | collective-permute-done | bytes 294944 | tf_op jit(solution)/shard_map/ppermute | solution.py:301
  323.2 2.4 fusion.29
  331.3 5.0 collective-permute-done.76
  336.4 13.4 %collective-permute-done.58 = bf16[96,768]{1,0:T(8,128)(2,1)S(1)} collective-permute-done((bf16[96,768]{1,0:T(8,128)(2,1)S(1)}, bf16[96,768]{1,0:T(8,128)(2,1)S(1)}, u32[]{:S(2)}, u32[]{:S(2)}) %collective-permute-start.58) | collective-permute-done | bytes 147488 | tf_op jit(solution)/shard_map/ppermute | solution.py:301
  352.0 2.7 collective-permute-done.77
  356.5 2.6 collective-permute-start.78
  359.1 2.5 collective-permute-done.78
  361.6 2.4 collective-permute-start.60
  364.0 2.7 collective-permute-done.60
  368.9 2.7 collective-permute-done.79
  373.7 2.7 collective-permute-done.61
  376.4 3.2 collective-permute-start.80
  379.7 2.3 collective-permute-done.80
  392.2 2.3 all_to_all.24
  402.3 8.8 %collective-permute-done.52 = bf16[96,576]{1,0:T(8,128)(2,1)S(1)} collective-permute-done((bf16[96,576]{1,0:T(8,128)(2,1)S(1)}, bf16[96,576]{1,0:T(8,128)(2,1)S(1)}, u32[]{:S(2)}, u32[]{:S(2)}) %collective-permute-start.52) | collective-permute-done | bytes 110624 | tf_op jit(solution)/shard_map/ppermute | solution.py:301
  411.2 4.1 collective-permute-done.45
  415.3 2.5 collective-permute-start.53
  421.9 3.2 collective-permute-done.46
  430.1 3.0 collective-permute-start.54
  434.6 2.3 fusion.15
  442.2 8.9 %collective-permute-done.70 = bf16[96,576]{1,0:T(8,128)(2,1)S(1)} collective-permute-done((bf16[96,576]{1,0:T(8,128)(2,1)S(1)}, bf16[96,576]{1,0:T(8,128)(2,1)S(1)}, u32[]{:S(2)}, u32[]{:S(2)}) %collective-permute-start.70) | collective-permute-done | bytes 110624 | tf_op jit(solution)/shard_map/ppermute | solution.py:301
  451.1 3.5 collective-permute-start.71
  456.5 9.1 %collective-permute-done.86 = bf16[192,768]{1,0:T(8,128)(2,1)S(1)} collective-permute-done((bf16[192,768]{1,0:T(8,128)(2,1)S(1)}, bf16[192,768]{1,0:T(8,128)(2,1)S(1)}, u32[]{:S(2)}, u32[]{:S(2)}) %collective-permute-start.86) | collective-permute-done | bytes 294944 | tf_op jit(solution)/shard_map/ppermute | solution.py:301
  468.0 8.3 %collective-permute-done.87 = bf16[192,768]{1,0:T(8,128)(2,1)S(1)} collective-permute-done((bf16[192,768]{1,0:T(8,128)(2,1)S(1)}, bf16[192,768]{1,0:T(8,128)(2,1)S(1)}, u32[]{:S(2)}, u32[]{:S(2)}) %collective-permute-start.87) | collective-permute-done | bytes 294944 | tf_op jit(solution)/shard_map/ppermute | solution.py:301
  480.2 6.2 %collective-permute-done.88 = bf16[384,768]{1,0:T(8,128)(2,1)S(1)} collective-permute-done((bf16[384,768]{1,0:T(8,128)(2,1)S(1)}, bf16[384,768]{1,0:T(8,128)(2,1)S(1)}, u32[]{:S(2)}, u32[]{:S(2)}) %collective-permute-start.88) | collective-permute-done | bytes 589856 | tf_op jit(solution)/shard_map/ppermute | solution.py:301
  497.4 7.0 %collective-permute-done.89 = bf16[768,768]{1,0:T(8,128)(2,1)} collective-permute-done((bf16[768,768]{1,0:T(8,128)(2,1)}, bf16[768,768]{1,0:T(8,128)(2,1)}, u32[]{:S(2)}, u32[]{:S(2)}) %collective-permute-start.89) | collective-permute-done | bytes 1179680 | tf_op jit(solution)/shard_map/ppermute | solution.py:301
  506.6 2.5 fusion.90
  (664 shorter events, 207.3 us)
Async XLA Ops:
  6.4 63.8 %collective-permute-start = (bf16[196,768]{1,0:T(8,128)(2,1)}, bf16[196,768]{1,0:T(8,128)(2,1)}, u32[]{:S(2)}, u32[]{:S(2)}) collective-permute-start(bf16[196,768]{1,0:T(8,128)(2,1)} %bitcast.148), channel_id=1, source_target_pairs={{0,1},{1,0},{2,3},{3,2},{4,5},{5,4},{6,7},{7,6},{8,9},{9,8},{10,11... | collective-permute-start | bytes 903176 | tf_op jit(solution)/shard_map/ppermute | solution.py:301
  6.9 69.7 %collective-permute-start.2 = (bf16[196,768]{1,0:T(8,128)(2,1)}, bf16[196,768]{1,0:T(8,128)(2,1)}, u32[]{:S(2)}, u32[]{:S(2)}) collective-permute-start(bf16[196,768]{1,0:T(8,128)(2,1)} %bitcast.148), channel_id=1, source_target_pairs={{0,3},{1,2},{2,1},{3,0},{4,7},{5,6},{6,5},{7,4},{8,11},{9,10},{10,... | collective-permute-start | bytes 903176 | tf_op jit(solution)/shard_map/ppermute | solution.py:301
  9.5 45.5 %collective-permute-start.8 = (bf16[192,768]{1,0:T(8,128)(2,1)}, bf16[192,768]{1,0:T(8,128)(2,1)}, u32[]{:S(2)}, u32[]{:S(2)}) collective-permute-start(bf16[192,768]{1,0:T(8,128)(2,1)} %param.45), channel_id=1, source_target_pairs={{0,2},{1,3},{2,0},{3,1},{4,6},{5,7},{6,4},{7,5},{8,10},{9,11},{10,... | collective-permute-start | bytes 884744 | tf_op jit(solution)/shard_map/ppermute | solution.py:301
  9.5 42.9 %collective-permute-start.7 = (bf16[192,768]{1,0:T(8,128)(2,1)}, bf16[192,768]{1,0:T(8,128)(2,1)}, u32[]{:S(2)}, u32[]{:S(2)}) collective-permute-start(bf16[192,768]{1,0:T(8,128)(2,1)} %param.45), channel_id=1, source_target_pairs={{0,1},{1,0},{2,3},{3,2},{4,5},{5,4},{6,7},{7,6},{8,9},{9,8},{10,11... | collective-permute-start | bytes 884744 | tf_op jit(solution)/shard_map/ppermute | solution.py:301
  9.6 20.8 %collective-permute-start.5 = (f32[3]{0:T(128)S(1)}, f32[3]{0:T(128)S(1)}, u32[]{:S(2)}, u32[]{:S(2)}) collective-permute-start(f32[3]{0:T(128)S(1)} %copy-done.110), channel_id=1, source_target_pairs={{0,1},{1,0},{2,3},{3,2},{4,5},{5,4},{6,7},{7,6},{8,9},{9,8},{10,11... | collective-permute-start | bytes 44 | tf_op jit(solution)/shard_map/ppermute | solution.py:301
  11.0 77.0 %all-to-all-start = ((bf16[32,8,768]{2,0,1:T(8,128)(2,1)}), bf16[32,8,768]{2,0,1:T(8,128)(2,1)}, u32[]{:S(2)}, u32[]{:S(2)}) async-start(bf16[32,8,768]{2,0,1:T(8,128)(2,1)} %dynamic-slice_bitcast_fusion), calls=%async_computation | async-start | bytes 786432 | tf_op jit(solution)/shard_map/all_to_all | solution.py:465
  52.4 9.4 %collective-permute-start.11 = (bf16[768,192]{0,1:T(8,128)(2,1)S(1)}, bf16[768,192]{0,1:T(8,128)(2,1)S(1)}, u32[]{:S(2)}, u32[]{:S(2)}) collective-permute-start(bf16[768,192]{0,1:T(8,128)(2,1)S(1)} %copy-done.76), channel_id=1, source_target_pairs={{0,2},{1,3},{2,0},{3,1},{4,6},{5,7},{6,4},{7,5},{8,10},{9,11},{10,... | collective-permute-start | bytes 884744 | tf_op jit(solution)/shard_map/ppermute | solution.py:301
  54.9 8.3 %collective-permute-start.17 = (bf16[768,192]{0,1:T(8,128)(2,1)S(1)}, bf16[768,192]{0,1:T(8,128)(2,1)S(1)}, u32[]{:S(2)}, u32[]{:S(2)}) collective-permute-start(bf16[768,192]{0,1:T(8,128)(2,1)S(1)} %copy-done.77), channel_id=1, source_target_pairs={{0,1},{1,0},{2,3},{3,2},{4,5},{5,4},{6,7},{7,6},{8,9},{9,8},{10,11... | collective-permute-start | bytes 884744 | tf_op jit(solution)/shard_map/ppermute | solution.py:301
  56.2 7.2 %collective-permute-start.19 = (bf16[192,768]{1,0:T(8,128)(2,1)S(1)}, bf16[192,768]{1,0:T(8,128)(2,1)S(1)}, u32[]{:S(2)}, u32[]{:S(2)}) collective-permute-start(bf16[192,768]{1,0:T(8,128)(2,1)S(1)} %copy-done.78), channel_id=1, source_target_pairs={{0,1},{1,0},{2,3},{3,2},{4,5},{5,4},{6,7},{7,6},{8,9},{9,8},{10,11... | collective-permute-start | bytes 884744 | tf_op jit(solution)/shard_map/ppermute | solution.py:301
  61.7 8.5 %collective-permute-start.20 = (bf16[192,768]{1,0:T(8,128)(2,1)S(1)}, bf16[192,768]{1,0:T(8,128)(2,1)S(1)}, u32[]{:S(2)}, u32[]{:S(2)}) collective-permute-start(bf16[192,768]{1,0:T(8,128)(2,1)S(1)} %copy-done.78), channel_id=1, source_target_pairs={{0,2},{1,3},{2,0},{3,1},{4,6},{5,7},{6,4},{7,5},{8,10},{9,11},{10,... | collective-permute-start | bytes 884744 | tf_op jit(solution)/shard_map/ppermute | solution.py:301
  63.2 70.2 %collective-permute-start.23 = (bf16[768,768]{1,0:T(8,128)(2,1)}, bf16[768,768]{1,0:T(8,128)(2,1)}, u32[]{:S(2)}, u32[]{:S(2)}) collective-permute-start(bf16[768,768]{1,0:T(8,128)(2,1)} %param.60), channel_id=1, source_target_pairs={{0,1},{1,0},{2,3},{3,2},{4,5},{5,4},{6,7},{7,6},{8,9},{9,8},{10,11... | collective-permute-start | bytes 3538952 | tf_op jit(solution)/shard_map/ppermute | solution.py:301
  63.4 7.5 %collective-permute-start.24 = (bf16[196,768]{1,0:T(8,128)(2,1)}, bf16[196,768]{1,0:T(8,128)(2,1)S(1)}, u32[]{:S(2)}, u32[]{:S(2)}) collective-permute-start(bf16[196,768]{1,0:T(8,128)(2,1)} %bitcast.147), channel_id=1, source_target_pairs={{0,1},{1,0},{2,3},{3,2},{4,5},{5,4},{6,7},{7,6},{8,9},{9,8},{10,11... | collective-permute-start | bytes 903176 | tf_op jit(solution)/shard_map/ppermute | solution.py:301
  74.1 10.3 %collective-permute-start.1 = (bf16[196,768]{1,0:T(8,128)(2,1)S(1)}, bf16[196,768]{1,0:T(8,128)(2,1)S(1)}, u32[]{:S(2)}, u32[]{:S(2)}) collective-permute-start(bf16[196,768]{1,0:T(8,128)(2,1)S(1)} %get-tuple-element.215), channel_id=1, source_target_pairs={{0,2},{1,3},{2,0},{3,1},{4,6},{5,7},{6,4},{7,5},{8,10},{9,11},{10,... | collective-permute-start | bytes 903176 | tf_op jit(solution)/shard_map/ppermute | solution.py:301
  75.7 56.6 %collective-permute-start.26 = (bf16[196,768]{1,0:T(8,128)(2,1)}, bf16[196,768]{1,0:T(8,128)(2,1)}, u32[]{:S(2)}, u32[]{:S(2)}) collective-permute-start(bf16[196,768]{1,0:T(8,128)(2,1)} %bitcast.147), channel_id=1, source_target_pairs={{0,3},{1,2},{2,1},{3,0},{4,7},{5,6},{6,5},{7,4},{8,11},{9,10},{10,... | collective-permute-start | bytes 903176 | tf_op jit(solution)/shard_map/ppermute | solution.py:301
  75.8 59.2 %collective-permute-start.27 = (bf16[768,768]{1,0:T(8,128)(2,1)}, bf16[768,768]{1,0:T(8,128)(2,1)}, u32[]{:S(2)}, u32[]{:S(2)}) collective-permute-start(bf16[768,768]{1,0:T(8,128)(2,1)} %param.63), channel_id=1, source_target_pairs={{0,1},{1,0},{2,3},{3,2},{4,5},{5,4},{6,7},{7,6},{8,9},{9,8},{10,11... | collective-permute-start | bytes 3538952 | tf_op jit(solution)/shard_map/ppermute | solution.py:301
  76.6 13.3 %collective-permute-start.3 = (bf16[3,768,192]{1,2,0:T(8,128)(2,1)}, bf16[3,768,192]{1,2,0:T(8,128)(2,1)}, u32[]{:S(2)}, u32[]{:S(2)}) collective-permute-start(bf16[3,768,192]{1,2,0:T(8,128)(2,1)} %pad_maximum_fusion.7), channel_id=1, source_target_pairs={{0,1},{1,0},{2,3},{3,2},{4,5},{5,4},{6,7},{7,6},{8,9},{9,8},{10,11... | collective-permute-start | bytes 2654216 | tf_op jit(solution)/shard_map/ppermute | solution.py:301
  84.4 48.0 %collective-permute-start.25 = (bf16[196,768]{1,0:T(8,128)(2,1)}, bf16[196,768]{1,0:T(8,128)(2,1)}, u32[]{:S(2)}, u32[]{:S(2)}) collective-permute-start(bf16[196,768]{1,0:T(8,128)(2,1)} %get-tuple-element.209), channel_id=1, source_target_pairs={{0,2},{1,3},{2,0},{3,1},{4,6},{5,7},{6,4},{7,5},{8,10},{9,11},{10,... | collective-permute-start | bytes 903176 | tf_op jit(solution)/shard_map/ppermute | solution.py:301
  89.9 22.2 %collective-permute-start.18 = (bf16[256,768]{1,0:T(8,128)(2,1)S(1)}, bf16[256,768]{1,0:T(8,128)(2,1)S(1)}, u32[]{:S(2)}, u32[]{:S(2)}) collective-permute-start(bf16[256,768]{1,0:T(8,128)(2,1)S(1)} %convolution_convert_fusion.6), channel_id=1, source_target_pairs={{0,2},{1,3},{2,0},{3,1},{4,6},{5,7},{6,4},{7,5},{8,10},{9,11},{10,... | collective-permute-start | bytes 1179656 | tf_op jit(solution)/shard_map/ppermute | solution.py:301
  112.1 6.9 %collective-permute-start.6 = (bf16[392,384]{1,0:T(8,128)(2,1)S(1)}, bf16[392,384]{1,0:T(8,128)(2,1)S(1)}, u32[]{:S(2)}, u32[]{:S(2)}) collective-permute-start(bf16[392,384]{1,0:T(8,128)(2,1)S(1)} %get-tuple-element.268), channel_id=1, source_target_pairs={{0,2},{1,3},{2,0},{3,1},{4,6},{5,7},{6,4},{7,5},{8,10},{9,11},{10,... | collective-permute-start | bytes 903176 | tf_op jit(solution)/shard_map/ppermute | solution.py:301
  131.0 10.3 %collective-permute-start.22 = (bf16[392,768]{1,0:T(8,128)(2,1)S(1)}, bf16[392,768]{1,0:T(8,128)(2,1)S(1)}, u32[]{:S(2)}, u32[]{:S(2)}) collective-permute-start(bf16[392,768]{1,0:T(8,128)(2,1)S(1)} %add_convert_fusion.1), channel_id=1, source_target_pairs={{0,2},{1,3},{2,0},{3,1},{4,6},{5,7},{6,4},{7,5},{8,10},{9,11},{10,... | collective-permute-start | bytes 1806344 | tf_op jit(solution)/shard_map/ppermute | solution.py:301
  162.2 108.7 %collective-permute-start.83 = (bf16[768,768]{1,0:T(8,128)(2,1)}, bf16[768,768]{1,0:T(8,128)(2,1)}, u32[]{:S(2)}, u32[]{:S(2)}) collective-permute-start(bf16[768,768]{1,0:T(8,128)(2,1)} %slice.640), channel_id=1, source_target_pairs={{0,1},{1,0},{2,3},{3,2},{4,5},{5,4},{6,7},{7,6},{8,9},{9,8},{10,11... | collective-permute-start | bytes 3538952 | tf_op jit(solution)/shard_map/ppermute | solution.py:301
  164.2 16.6 %collective-permute-start.32 = (bf16[392,768]{1,0:T(8,128)(2,1)S(1)}, bf16[392,768]{1,0:T(8,128)(2,1)S(1)}, u32[]{:S(2)}, u32[]{:S(2)}) collective-permute-start(bf16[392,768]{1,0:T(8,128)(2,1)S(1)} %convolution_convert_fusion.1), channel_id=1, source_target_pairs={{0,2},{1,3},{2,0},{3,1},{4,6},{5,7},{6,4},{7,5},{8,10},{9,11},{10,... | collective-permute-start | bytes 1806344 | tf_op jit(solution)/shard_map/ppermute | solution.py:301
  171.3 102.1 %collective-permute-start.82 = (bf16[768,768]{1,0:T(8,128)(2,1)}, bf16[768,768]{1,0:T(8,128)(2,1)}, u32[]{:S(2)}, u32[]{:S(2)}) collective-permute-start(bf16[768,768]{1,0:T(8,128)(2,1)} %slice.641), channel_id=1, source_target_pairs={{0,1},{1,0},{2,3},{3,2},{4,5},{5,4},{6,7},{7,6},{8,9},{9,8},{10,11... | collective-permute-start | bytes 3538952 | tf_op jit(solution)/shard_map/ppermute | solution.py:301
  171.3 37.2 %collective-permute-start.30 = (bf16[392,768]{1,0:T(8,128)(2,1)}, bf16[392,768]{1,0:T(8,128)(2,1)}, u32[]{:S(2)}, u32[]{:S(2)}) collective-permute-start(bf16[392,768]{1,0:T(8,128)(2,1)} %convolution_convert_fusion.2), channel_id=1, source_target_pairs={{0,2},{1,3},{2,0},{3,1},{4,6},{5,7},{6,4},{7,5},{8,10},{9,11},{10,... | collective-permute-start | bytes 1806344 | tf_op jit(solution)/shard_map/ppermute | solution.py:301
  200.3 78.2 %collective-permute-start.74 = (bf16[384,768]{1,0:T(8,128)(2,1)}, bf16[384,768]{1,0:T(8,128)(2,1)}, u32[]{:S(2)}, u32[]{:S(2)}) collective-permute-start(bf16[384,768]{1,0:T(8,128)(2,1)} %pad_maximum_fusion.17), channel_id=1, source_target_pairs={{0,1},{1,0},{2,3},{3,2},{4,5},{5,4},{6,7},{7,6},{8,9},{9,8},{10,11... | collective-permute-start | bytes 1769480 | tf_op jit(solution)/shard_map/ppermute | solution.py:301
  200.7 12.9 %collective-permute-start.37 = (bf16[256,384]{1,0:T(8,128)(2,1)S(1)}, bf16[256,384]{1,0:T(8,128)(2,1)S(1)}, u32[]{:S(2)}, u32[]{:S(2)}) collective-permute-start(bf16[256,384]{1,0:T(8,128)(2,1)S(1)} %slice.643), channel_id=1, source_target_pairs={{0,2},{1,3},{2,0},{3,1},{4,6},{5,7},{6,4},{7,5},{8,10},{9,11},{10,... | collective-permute-start | bytes 589832 | tf_op jit(solution)/shard_map/ppermute | solution.py:301
  208.5 7.1 %collective-permute-start.38 = (bf16[256,384]{1,0:T(8,128)(2,1)S(1)}, bf16[256,384]{1,0:T(8,128)(2,1)S(1)}, u32[]{:S(2)}, u32[]{:S(2)}) collective-permute-start(bf16[256,384]{1,0:T(8,128)(2,1)S(1)} %slice.642), channel_id=1, source_target_pairs={{0,2},{1,3},{2,0},{3,1},{4,6},{5,7},{6,4},{7,5},{8,10},{9,11},{10,... | collective-permute-start | bytes 589832 | tf_op jit(solution)/shard_map/ppermute | solution.py:301
  213.6 9.1 %collective-permute-start.34 = (bf16[392,384]{1,0:T(8,128)(2,1)S(1)}, bf16[392,384]{1,0:T(8,128)(2,1)S(1)}, u32[]{:S(2)}, u32[]{:S(2)}) collective-permute-start(bf16[392,384]{1,0:T(8,128)(2,1)S(1)} %slice.487), channel_id=1, source_target_pairs={{0,2},{1,3},{2,0},{3,1},{4,6},{5,7},{6,4},{7,5},{8,10},{9,11},{10,... | collective-permute-start | bytes 903176 | tf_op jit(solution)/shard_map/ppermute | solution.py:301
  215.6 38.3 %collective-permute-start.31 = (bf16[196,768]{1,0:T(8,128)(2,1)}, bf16[196,768]{1,0:T(8,128)(2,1)}, u32[]{:S(2)}, u32[]{:S(2)}) collective-permute-start(bf16[196,768]{1,0:T(8,128)(2,1)} %constant_dynamic-slice_fusion.2), channel_id=1, source_target_pairs={{0,1},{1,0},{2,3},{3,2},{4,5},{5,4},{6,7},{7,6},{8,9},{9,8},{10,11... | collective-permute-start | bytes 903176 | tf_op jit(solution)/shard_map/ppermute | solution.py:301
  222.7 44.4 %collective-permute-start.66 = (bf16[768,192]{1,0:T(8,128)(2,1)}, bf16[768,192]{1,0:T(8,128)(2,1)}, u32[]{:S(2)}, u32[]{:S(2)}) collective-permute-start(bf16[768,192]{1,0:T(8,128)(2,1)} %get-tuple-element.246), channel_id=1, source_target_pairs={{0,1},{1,0},{2,3},{3,2},{4,5},{5,4},{6,7},{7,6},{8,9},{9,8},{10,11... | collective-permute-start | bytes 884744 | tf_op jit(solution)/shard_map/ppermute | solution.py:301
  258.8 7.1 %collective-permute-start.39 = (bf16[256,384]{1,0:T(8,128)(2,1)}, bf16[256,384]{1,0:T(8,128)(2,1)S(1)}, u32[]{:S(2)}, u32[]{:S(2)}) collective-permute-start(bf16[256,384]{1,0:T(8,128)(2,1)} %dynamic-slice_convert_fusion.6), channel_id=1, source_target_pairs={{0,2},{1,3},{2,0},{3,1},{4,6},{5,7},{6,4},{7,5},{8,10},{9,11},{10,... | collective-permute-start | bytes 589832 | tf_op jit(solution)/shard_map/ppermute | solution.py:301
  267.2 12.6 %collective-permute-start.64 = (bf16[768,384]{1,0:T(8,128)(2,1)S(1)}, bf16[768,384]{1,0:T(8,128)(2,1)S(1)}, u32[]{:S(2)}, u32[]{:S(2)}) collective-permute-start(bf16[768,384]{1,0:T(8,128)(2,1)S(1)} %copy-done.69), channel_id=1, source_target_pairs={{0,1},{1,0},{2,3},{3,2},{4,5},{5,4},{6,7},{7,6},{8,9},{9,8},{10,11... | collective-permute-start | bytes 1769480 | tf_op jit(solution)/shard_map/ppermute | solution.py:301
  267.9 17.6 %collective-permute-start.56 = (bf16[384,768]{1,0:T(8,128)(2,1)S(1)}, bf16[384,768]{1,0:T(8,128)(2,1)S(1)}, u32[]{:S(2)}, u32[]{:S(2)}) collective-permute-start(bf16[384,768]{1,0:T(8,128)(2,1)S(1)} %copy-done.68), channel_id=1, source_target_pairs={{0,1},{1,0},{2,3},{3,2},{4,5},{5,4},{6,7},{7,6},{8,9},{9,8},{10,11... | collective-permute-start | bytes 1769480 | tf_op jit(solution)/shard_map/ppermute | solution.py:301
  270.9 25.6 %collective-permute-start.47 = (bf16[768,192]{1,0:T(8,128)(2,1)}, bf16[768,192]{1,0:T(8,128)(2,1)}, u32[]{:S(2)}, u32[]{:S(2)}) collective-permute-start(bf16[768,192]{1,0:T(8,128)(2,1)} %get-tuple-element.235), channel_id=1, source_target_pairs={{0,1},{1,0},{2,3},{3,2},{4,5},{5,4},{6,7},{7,6},{8,9},{9,8},{10,11... | collective-permute-start | bytes 884744 | tf_op jit(solution)/shard_map/ppermute | solution.py:301
  273.5 24.0 %collective-permute-start.48 = (bf16[768,192]{1,0:T(8,128)(2,1)}, bf16[768,192]{1,0:T(8,128)(2,1)}, u32[]{:S(2)}, u32[]{:S(2)}) collective-permute-start(bf16[768,192]{1,0:T(8,128)(2,1)} %get-tuple-element.237), channel_id=1, source_target_pairs={{0,1},{1,0},{2,3},{3,2},{4,5},{5,4},{6,7},{7,6},{8,9},{9,8},{10,11... | collective-permute-start | bytes 884744 | tf_op jit(solution)/shard_map/ppermute | solution.py:301
  278.5 20.1 %collective-permute-start.49 = (bf16[768,192]{1,0:T(8,128)(2,1)S(1)}, bf16[768,192]{1,0:T(8,128)(2,1)}, u32[]{:S(2)}, u32[]{:S(2)}) collective-permute-start(bf16[768,192]{1,0:T(8,128)(2,1)S(1)} %get-tuple-element.236), channel_id=1, source_target_pairs={{0,1},{1,0},{2,3},{3,2},{4,5},{5,4},{6,7},{7,6},{8,9},{9,8},{10,11... | collective-permute-start | bytes 884744 | tf_op jit(solution)/shard_map/ppermute | solution.py:301
  279.8 43.4 %collective-permute-start.35 = (bf16[392,768]{1,0:T(8,128)(2,1)}, bf16[392,768]{1,0:T(8,128)(2,1)}, u32[]{:S(2)}, u32[]{:S(2)}) collective-permute-start(bf16[392,768]{1,0:T(8,128)(2,1)} %convolution_convert_fusion.3), channel_id=1, source_target_pairs={{0,2},{1,3},{2,0},{3,1},{4,6},{5,7},{6,4},{7,5},{8,10},{9,11},{10,... | collective-permute-start | bytes 1806344 | tf_op jit(solution)/shard_map/ppermute | solution.py:301
  288.0 146.5 %collective-permute-start.84 = (bf16[768,768]{1,0:T(8,128)(2,1)}, bf16[768,768]{1,0:T(8,128)(2,1)}, u32[]{:S(2)}, u32[]{:S(2)}) collective-permute-start(bf16[768,768]{1,0:T(8,128)(2,1)} %fusion.13), channel_id=1, source_target_pairs={{0,4},{4,0},{8,12},{12,8},{16,20},{20,16},{24,28},{28,24},{1,5},{5... | collective-permute-start | bytes 3538952 | tf_op jit(solution)/shard_map/ppermute | solution.py:301
  291.5 98.5 %all-to-all-start.1 = ((f32[256,2,192]{2,1,0:T(2,128)}), f32[256,2,192]{2,1,0:T(2,128)}, u32[]{:S(2)}, u32[]{:S(2)}) async-start(f32[256,2,192]{2,1,0:T(2,128)} %copy.131), calls=%async_computation.1 | async-start | bytes 1048576 | tf_op jit(solution)/shard_map/all_to_all | solution.py:669
  296.5 10.2 %collective-permute-start.75 = (bf16[192,768]{1,0:T(8,128)(2,1)}, bf16[192,768]{1,0:T(8,128)(2,1)S(1)}, u32[]{:S(2)}, u32[]{:S(2)}) collective-permute-start(bf16[192,768]{1,0:T(8,128)(2,1)} %fusion.46), channel_id=1, source_target_pairs={{0,2},{1,3},{2,0},{3,1},{4,6},{5,7},{6,4},{7,5},{8,10},{9,11},{10,... | collective-permute-start | bytes 884744 | tf_op jit(solution)/shard_map/ppermute | solution.py:301
  297.5 17.6 %collective-permute-start.65 = (bf16[768,192]{1,0:T(8,128)(2,1)}, bf16[768,192]{1,0:T(8,128)(2,1)S(1)}, u32[]{:S(2)}, u32[]{:S(2)}) collective-permute-start(bf16[768,192]{1,0:T(8,128)(2,1)} %fusion.38), channel_id=1, source_target_pairs={{0,2},{1,3},{2,0},{3,1},{4,6},{5,7},{6,4},{7,5},{8,10},{9,11},{10,... | collective-permute-start | bytes 884744 | tf_op jit(solution)/shard_map/ppermute | solution.py:301
  298.6 21.6 %collective-permute-start.57 = (bf16[192,768]{1,0:T(8,128)(2,1)}, bf16[192,768]{1,0:T(8,128)(2,1)S(1)}, u32[]{:S(2)}, u32[]{:S(2)}) collective-permute-start(bf16[192,768]{1,0:T(8,128)(2,1)} %fusion.48), channel_id=1, source_target_pairs={{0,2},{1,3},{2,0},{3,1},{4,6},{5,7},{6,4},{7,5},{8,10},{9,11},{10,... | collective-permute-start | bytes 884744 | tf_op jit(solution)/shard_map/ppermute | solution.py:301
  306.7 44.9 %collective-permute-start.50 = (bf16[384,576]{1,0:T(8,128)(2,1)S(1)}, bf16[384,576]{1,0:T(8,128)(2,1)S(1)}, u32[]{:S(2)}, u32[]{:S(2)}) collective-permute-start(bf16[384,576]{1,0:T(8,128)(2,1)S(1)} %dynamic-slice_convert_fusion.2), channel_id=1, source_target_pairs={{0,4},{4,0},{8,12},{12,8},{16,20},{20,16},{24,28},{28,24},{1,5},{5... | collective-permute-start | bytes 1327112 | tf_op jit(solution)/shard_map/ppermute | solution.py:301
  315.1 21.2 %collective-permute-start.76 = (bf16[96,768]{1,0:T(8,128)(2,1)S(1)}, bf16[96,768]{1,0:T(8,128)(2,1)S(1)}, u32[]{:S(2)}, u32[]{:S(2)}) collective-permute-start(bf16[96,768]{1,0:T(8,128)(2,1)S(1)} %dynamic-slice_convert_fusion.7), channel_id=1, source_target_pairs={{0,4},{4,0},{8,12},{12,8},{16,20},{20,16},{24,28},{28,24},{1,5},{5... | collective-permute-start | bytes 442376 | tf_op jit(solution)/shard_map/ppermute | solution.py:301
  320.2 77.0 %collective-permute-start.68 = (bf16[384,576]{1,0:T(8,128)(2,1)}, bf16[384,576]{1,0:T(8,128)(2,1)}, u32[]{:S(2)}, u32[]{:S(2)}) collective-permute-start(bf16[384,576]{1,0:T(8,128)(2,1)} %dynamic-slice_convert_fusion.1), channel_id=1, source_target_pairs={{0,4},{4,0},{8,12},{12,8},{16,20},{20,16},{24,28},{28,24},{1,5},{5... | collective-permute-start | bytes 1327112 | tf_op jit(solution)/shard_map/ppermute | solution.py:301
  331.0 18.8 %collective-permute-start.58 = (bf16[96,768]{1,0:T(8,128)(2,1)S(1)}, bf16[96,768]{1,0:T(8,128)(2,1)S(1)}, u32[]{:S(2)}, u32[]{:S(2)}) collective-permute-start(bf16[96,768]{1,0:T(8,128)(2,1)S(1)} %dynamic-slice_convert_fusion.8), channel_id=1, source_target_pairs={{0,4},{4,0},{8,12},{12,8},{16,20},{20,16},{24,28},{28,24},{1,5},{5... | collective-permute-start | bytes 442376 | tf_op jit(solution)/shard_map/ppermute | solution.py:301
  336.3 96.8 %collective-permute-start.36 = (f32[196,768]{1,0:T(8,128)}, f32[196,768]{1,0:T(8,128)}, u32[]{:S(2)}, u32[]{:S(2)}) collective-permute-start(f32[196,768]{1,0:T(8,128)} %constant_dynamic-slice_fusion.1), channel_id=1, source_target_pairs={{0,1},{1,0},{2,3},{3,2},{4,5},{5,4},{6,7},{7,6},{8,9},{9,8},{10,11... | collective-permute-start | bytes 1806344 | tf_op jit(solution)/shard_map/ppermute | solution.py:301
  354.7 33.8 %collective-permute-start.51 = (bf16[192,576]{1,0:T(8,128)(2,1)S(1)}, bf16[192,576]{1,0:T(8,128)(2,1)S(1)}, u32[]{:S(2)}, u32[]{:S(2)}) collective-permute-start(bf16[192,576]{1,0:T(8,128)(2,1)S(1)} %dynamic-slice_convert_fusion.5), channel_id=1, source_target_pairs={{0,8},{4,12},{8,0},{12,4},{16,24},{20,28},{24,16},{28,20},{1,9},{5... | collective-permute-start | bytes 663560 | tf_op jit(solution)/shard_map/ppermute | solution.py:301
  386.4 28.9 %collective-permute-start.81 = (bf16[96,768]{1,0:T(8,128)(2,1)}, bf16[96,768]{1,0:T(8,128)(2,1)}, u32[]{:S(2)}, u32[]{:S(2)}) collective-permute-start(bf16[96,768]{1,0:T(8,128)(2,1)} %pad_maximum_fusion.34), channel_id=1, source_target_pairs={{0,4},{4,0},{8,12},{12,8},{16,20},{20,16},{24,28},{28,24},{1,5},{5... | collective-permute-start | bytes 442376 | tf_op jit(solution)/shard_map/ppermute | solution.py:301
  388.5 31.1 %collective-permute-start.63 = (bf16[96,768]{1,0:T(8,128)(2,1)}, bf16[96,768]{1,0:T(8,128)(2,1)}, u32[]{:S(2)}, u32[]{:S(2)}) collective-permute-start(bf16[96,768]{1,0:T(8,128)(2,1)} %pad_maximum_fusion.33), channel_id=1, source_target_pairs={{0,4},{4,0},{8,12},{12,8},{16,20},{20,16},{24,28},{28,24},{1,5},{5... | collective-permute-start | bytes 442376 | tf_op jit(solution)/shard_map/ppermute | solution.py:301
  401.3 9.8 %collective-permute-start.52 = (bf16[96,576]{1,0:T(8,128)(2,1)S(1)}, bf16[96,576]{1,0:T(8,128)(2,1)S(1)}, u32[]{:S(2)}, u32[]{:S(2)}) collective-permute-start(bf16[96,576]{1,0:T(8,128)(2,1)S(1)} %dynamic-slice_convert_fusion.10), channel_id=1, source_target_pairs={{0,16},{4,20},{8,24},{12,28},{16,0},{20,4},{24,8},{28,12},{1,17},{... | collective-permute-start | bytes 331784 | tf_op jit(solution)/shard_map/ppermute | solution.py:301
  415.2 22.3 %collective-permute-start.69 = (bf16[192,576]{1,0:T(8,128)(2,1)S(1)}, bf16[192,576]{1,0:T(8,128)(2,1)}, u32[]{:S(2)}, u32[]{:S(2)}) collective-permute-start(bf16[192,576]{1,0:T(8,128)(2,1)S(1)} %dynamic-slice_convert_fusion.4), channel_id=1, source_target_pairs={{0,8},{4,12},{8,0},{12,4},{16,24},{20,28},{24,16},{28,20},{1,9},{5... | collective-permute-start | bytes 663560 | tf_op jit(solution)/shard_map/ppermute | solution.py:301
  415.3 13.9 %collective-permute-start.53 = (bf16[96,576]{1,0:T(8,128)(2,1)S(1)}, bf16[96,576]{1,0:T(8,128)(2,1)}, u32[]{:S(2)}, u32[]{:S(2)}) collective-permute-start(bf16[96,576]{1,0:T(8,128)(2,1)S(1)} %add_convert_fusion.7), channel_id=1, source_target_pairs={{0,16},{4,20},{8,24},{12,28},{16,0},{20,4},{24,8},{28,12},{1,17},{... | collective-permute-start | bytes 331784 | tf_op jit(solution)/shard_map/ppermute | solution.py:301
  430.1 24.7 %collective-permute-start.54 = (bf16[192,576]{1,0:T(8,128)(2,1)S(1)}, bf16[192,576]{1,0:T(8,128)(2,1)S(1)}, u32[]{:S(2)}, u32[]{:S(2)}) collective-permute-start(bf16[192,576]{1,0:T(8,128)(2,1)S(1)} %pad_maximum_fusion.29), channel_id=1, source_target_pairs={{0,8},{4,12},{8,0},{12,4},{16,24},{20,28},{24,16},{28,20},{1,9},{5... | collective-permute-start | bytes 663560 | tf_op jit(solution)/shard_map/ppermute | solution.py:301
  436.9 17.7 %collective-permute-start.85 = (bf16[384,768]{1,0:T(8,128)(2,1)S(1)}, bf16[384,768]{1,0:T(8,128)(2,1)S(1)}, u32[]{:S(2)}, u32[]{:S(2)}) collective-permute-start(bf16[384,768]{1,0:T(8,128)(2,1)S(1)} %dynamic-slice_convert_fusion), channel_id=1, source_target_pairs={{0,8},{4,12},{8,0},{12,4},{16,24},{20,28},{24,16},{28,20},{1,9},{5... | collective-permute-start | bytes 1769480 | tf_op jit(solution)/shard_map/ppermute | solution.py:301
  439.0 12.0 %collective-permute-start.70 = (bf16[96,576]{1,0:T(8,128)(2,1)S(1)}, bf16[96,576]{1,0:T(8,128)(2,1)S(1)}, u32[]{:S(2)}, u32[]{:S(2)}) collective-permute-start(bf16[96,576]{1,0:T(8,128)(2,1)S(1)} %dynamic-slice_convert_fusion.9), channel_id=1, source_target_pairs={{0,16},{4,20},{8,24},{12,28},{16,0},{20,4},{24,8},{28,12},{1,17},{... | collective-permute-start | bytes 331784 | tf_op jit(solution)/shard_map/ppermute | solution.py:301
  451.1 16.5 %collective-permute-start.71 = (bf16[96,576]{1,0:T(8,128)(2,1)S(1)}, bf16[96,576]{1,0:T(8,128)(2,1)S(1)}, u32[]{:S(2)}, u32[]{:S(2)}) collective-permute-start(bf16[96,576]{1,0:T(8,128)(2,1)S(1)} %add_convert_fusion.6), channel_id=1, source_target_pairs={{0,16},{4,20},{8,24},{12,28},{16,0},{20,4},{24,8},{28,12},{1,17},{... | collective-permute-start | bytes 331784 | tf_op jit(solution)/shard_map/ppermute | solution.py:301
  454.8 10.8 %collective-permute-start.86 = (bf16[192,768]{1,0:T(8,128)(2,1)S(1)}, bf16[192,768]{1,0:T(8,128)(2,1)S(1)}, u32[]{:S(2)}, u32[]{:S(2)}) collective-permute-start(bf16[192,768]{1,0:T(8,128)(2,1)S(1)} %dynamic-slice_convert_fusion.3), channel_id=1, source_target_pairs={{0,16},{4,20},{8,24},{12,28},{16,0},{20,4},{24,8},{28,12},{1,17},{... | collective-permute-start | bytes 884744 | tf_op jit(solution)/shard_map/ppermute | solution.py:301
  455.0 25.0 %collective-permute-start.55 = (bf16[384,576]{1,0:T(8,128)(2,1)S(1)}, bf16[384,576]{1,0:T(8,128)(2,1)S(1)}, u32[]{:S(2)}, u32[]{:S(2)}) collective-permute-start(bf16[384,576]{1,0:T(8,128)(2,1)S(1)} %pad_maximum_fusion.20), channel_id=1, source_target_pairs={{0,4},{4,0},{8,12},{12,8},{16,20},{20,16},{24,28},{28,24},{1,5},{5... | collective-permute-start | bytes 1327112 | tf_op jit(solution)/shard_map/ppermute | solution.py:301
  465.7 10.7 %collective-permute-start.87 = (bf16[192,768]{1,0:T(8,128)(2,1)S(1)}, bf16[192,768]{1,0:T(8,128)(2,1)S(1)}, u32[]{:S(2)}, u32[]{:S(2)}) collective-permute-start(bf16[192,768]{1,0:T(8,128)(2,1)S(1)} %add_convert_fusion.3), channel_id=1, source_target_pairs={{0,16},{4,20},{8,24},{12,28},{16,0},{20,4},{24,8},{28,12},{1,17},{... | collective-permute-start | bytes 884744 | tf_op jit(solution)/shard_map/ppermute | solution.py:301
  467.6 9.3 %collective-permute-start.72 = (bf16[192,576]{1,0:T(8,128)(2,1)S(1)}, bf16[192,576]{1,0:T(8,128)(2,1)S(1)}, u32[]{:S(2)}, u32[]{:S(2)}) collective-permute-start(bf16[192,576]{1,0:T(8,128)(2,1)S(1)} %pad_maximum_fusion.30), channel_id=1, source_target_pairs={{0,8},{4,12},{8,0},{12,4},{16,24},{20,28},{24,16},{28,20},{1,9},{5... | collective-permute-start | bytes 663560 | tf_op jit(solution)/shard_map/ppermute | solution.py:301
  476.5 9.9 %collective-permute-start.88 = (bf16[384,768]{1,0:T(8,128)(2,1)S(1)}, bf16[384,768]{1,0:T(8,128)(2,1)S(1)}, u32[]{:S(2)}, u32[]{:S(2)}) collective-permute-start(bf16[384,768]{1,0:T(8,128)(2,1)S(1)} %pad_maximum_fusion.18), channel_id=1, source_target_pairs={{0,8},{4,12},{8,0},{12,4},{16,24},{20,28},{24,16},{28,20},{1,9},{5... | collective-permute-start | bytes 1769480 | tf_op jit(solution)/shard_map/ppermute | solution.py:301
  478.6 13.9 %collective-permute-start.73 = (bf16[384,576]{1,0:T(8,128)(2,1)}, bf16[384,576]{1,0:T(8,128)(2,1)}, u32[]{:S(2)}, u32[]{:S(2)}) collective-permute-start(bf16[384,576]{1,0:T(8,128)(2,1)} %pad_maximum_fusion.21), channel_id=1, source_target_pairs={{0,4},{4,0},{8,12},{12,8},{16,20},{20,16},{24,28},{28,24},{1,5},{5... | collective-permute-start | bytes 1327112 | tf_op jit(solution)/shard_map/ppermute | solution.py:301
  487.9 16.5 %collective-permute-start.89 = (bf16[768,768]{1,0:T(8,128)(2,1)}, bf16[768,768]{1,0:T(8,128)(2,1)}, u32[]{:S(2)}, u32[]{:S(2)}) collective-permute-start(bf16[768,768]{1,0:T(8,128)(2,1)} %pad_maximum_fusion.6), channel_id=1, source_target_pairs={{0,4},{4,0},{8,12},{12,8},{16,20},{20,16},{24,28},{28,24},{1,5},{5... | collective-permute-start | bytes 3538952 | tf_op jit(solution)/shard_map/ppermute | solution.py:301
  (145 other events, 869.1 us)
